TPU v7x, 512 devices: a whole 4x8x8 slice. The times are simulated.
512 devices in a mesh: tile: 128 (over z, y, core), grp: 4 (over x).
Axes of the slice: x: 4, y: 8, z: 8, core: 2. Of those that a mesh axis runs over, the one named last changes fastest.
Arguments:
- kelvin_profile: float32 [90, 128, 256], P(None, 'tile'), may hold values from 0.5 to 1.5
- moisture_profile: float32 [90, 128, 256], P(None, 'tile'), may hold values from 0.1 to 3
- spreading_number: float32 [128, 256], P('tile'), may hold values from 0.05 to 0.24
- overhead_angle_measure: float32 [128, 256], P('tile'), may hold values from 0.2 to 1
- illuminated_mask: int32 [128, 256], P('tile'), may hold values 0 or 1
- radiating_tiles: int32 [32768, 1], P('tile'), may hold values from 0 to 127; in each aligned block of 256 rows (0 to 255, 256 to 511, ...) at most 4 rows name the same one
- cloudy_member_factors: float32 [224, 65536], P('grp', 'tile'), may hold values from 0.25 to 2
- arid_opacity_table: float32 [224, 90], P('grp'), may hold values from 0.003 to 0.2
- moisture_attenuation: float32 [224], P('grp'), may hold values from 0.003 to 0.05
- blackbody_share: float32 [224], P('grp'), may hold values from 0.3 to 3
- insolation_per_quadrature: float32 [224], P('grp'), may hold values from 0.3 to 3
Outputs:
- heating: float32 [90, 128, 256], P(None, 'tile')
- temp_next: float32 [90, 128, 256], P(None, 'tile')
- vapour_next: float32 [90, 128, 256], P(None, 'tile')
Inputs may be any that keep to these rules, and one draw needn't show every extreme that they name: `radiating_tiles`: among the columns of one tile no owner is named more than 4 times, a bound that some block reaches.
All inputs are finite; a program needn't handle non-finite values. No bound on the sum of `illuminated_mask` on one device may be relied on, other than what follows from the above.
Results may differ from a plain program's by a relative error of at most 0.00025.
Values sent between devices are 32-bit elements; how exact they have to be, the bound alone decides.
A program may use at most 64 MiB of HBM per device.

v0:
```python
import math

import jax
import jax.numpy as jnp
from jax import lax
from jax.sharding import PartitionSpec as P

NG = 224


def with_halo(block, sides, width):
    for axis, dim in sides:
        count = lax.axis_size(axis)
        forward = [(i, i + 1) for i in range(count - 1)]
        backward = [(target, source) for source, target in forward]
        low = lax.ppermute(
            lax.slice_in_dim(block, block.shape[dim] - width, None, axis=dim), axis, forward
        )
        high = lax.ppermute(lax.slice_in_dim(block, 0, width, axis=dim), axis, backward)
        block = jnp.concatenate([low, block, high], axis=dim)
    return block


def evaluate_warming(
    kelvin_profile,
    moisture_profile,
    overhead_angle_value,
    illuminated_marker,
    profile_window,
    arid_multiplier,
    moisture_multiplier,
    radiance_share_table,
    sunshine_multiplier,
):
    gpoints, strata_mesh = arid_multiplier.shape
    bundle = math.gcd(gpoints, 4)
    bundles = gpoints // bundle
    lower_mask = (jnp.arange(strata_mesh)[None, :] < jnp.arange(strata_mesh + 1)[:, None]).astype(
        jnp.float32
    )
    upper_mask = 1.0 - lower_mask

    def layer_pass(pieces):
        dry_part, vapour_part, radiance_share_piece, solar_part, sub_part = pieces
        thickness = (
            dry_part[:, :, None]
            + (vapour_part[:, None] * sub_part)[:, None, :] * moisture_profile[None]
        )
        column_depth = jnp.einsum(
            "lk,gkm->glm", lower_mask, thickness, precision=lax.Precision.HIGHEST
        )
        growth = jnp.exp(column_depth)
        damped = jnp.exp(-column_depth)
        infrared_radiance = radiance_share_piece[:, None, None] * kelvin_profile[None]
        downward = damped * jnp.einsum(
            "lk,gkm->glm",
            lower_mask,
            infrared_radiance * growth[:, :strata_mesh] * jnp.expm1(thickness),
            precision=lax.Precision.HIGHEST,
        )
        floor_term = infrared_radiance[:, strata_mesh - 1] * damped[:, strata_mesh]
        upward = growth * (
            floor_term[:, None, :]
            - jnp.einsum(
                "lk,gkm->glm",
                upper_mask,
                infrared_radiance * damped[:, :strata_mesh] * jnp.expm1(-thickness),
                precision=lax.Precision.HIGHEST,
            )
        )
        sunbeam = (
            solar_part[:, None, None]
            * illuminated_marker[None, None, :]
            * jnp.exp(-column_depth / overhead_angle_value[None, None, :])
        )
        fluxes = downward - upward + sunbeam
        return jnp.sum(fluxes[:, :strata_mesh] - fluxes[:, 1:], axis=0)

    spectral = lax.map(
        layer_pass,
        (
            arid_multiplier.reshape(bundles, bundle, strata_mesh),
            moisture_multiplier.reshape(bundles, bundle),
            radiance_share_table.reshape(bundles, bundle),
            sunshine_multiplier.reshape(bundles, bundle),
            profile_window.reshape(bundles, bundle, profile_window.shape[1]),
        ),
    )
    return jnp.sum(spectral, axis=0)


def advance(atmosphere_variables, spreading_number):
    padded = with_halo(atmosphere_variables, (("tile", 2),), 1)
    eastern = jnp.roll(atmosphere_variables, -1, axis=3)
    western = jnp.roll(atmosphere_variables, 1, axis=3)
    return atmosphere_variables + spreading_number * (
        padded[:, :, :-2] + padded[:, :, 2:] + eastern + western - 4.0 * atmosphere_variables
    )


def on_device(
    kelvin_profile,
    moisture_profile,
    spreading_number,
    overhead_angle_measure,
    illuminated_mask,
    radiating_tiles,
    cloudy_member_factors,
    arid_opacity_table,
    moisture_attenuation,
    blackbody_share,
    insolation_per_quadrature,
):
    strata_mesh, parallel_band_sequence, meridian_boxes = kelvin_profile.shape
    atmosphere_variables = jnp.stack([kelvin_profile, moisture_profile])
    for repeat in range(2):
        atmosphere_variables = advance(atmosphere_variables, spreading_number)
    temp_dyn = atmosphere_variables[0]
    vapour_next = atmosphere_variables[1]
    columns = parallel_band_sequence * meridian_boxes
    tile_count = lax.axis_size("tile")
    capacity = cloudy_member_factors.shape[1] // tile_count
    slots = tile_count * capacity
    owner_ids = radiating_tiles[:, 0]
    matches = (owner_ids[:, None] == jnp.arange(tile_count, dtype=jnp.int32)[None, :]).astype(
        jnp.int32
    )
    position = jnp.sum((jnp.cumsum(matches, axis=0) - 1) * matches, axis=1)
    slot_index = owner_ids * capacity + position
    overhead_angle_value = overhead_angle_measure.reshape(columns)
    sunlit_local = overhead_angle_value * illuminated_mask.reshape(columns).astype(jnp.float32)
    column_rows = jnp.concatenate(
        [temp_dyn.reshape(strata_mesh, columns).T, vapour_next.reshape(strata_mesh, columns).T],
        axis=1,
    )
    outgoing = (
        jnp.zeros((slots, 2 * strata_mesh), jnp.float32)
        .at[slot_index]
        .set(column_rows)
        .reshape(tile_count, capacity, 2 * strata_mesh)
    )
    sun_rows = jnp.stack([overhead_angle_value, sunlit_local], axis=1)
    blank = jnp.stack([jnp.ones((slots,), jnp.float32), jnp.zeros((slots,), jnp.float32)], axis=1)
    sun_out = blank.at[slot_index].set(sun_rows).reshape(tile_count, capacity, 2)
    incoming, sun_in = (
        lax.all_to_all(outgoing, "tile", split_axis=0, concat_axis=0, tiled=True),
        lax.all_to_all(sun_out, "tile", split_axis=0, concat_axis=0, tiled=True),
    )
    incoming = incoming.reshape(slots, 2 * strata_mesh)
    sun_in = sun_in.reshape(slots, 2)
    partial_value = evaluate_warming(
        incoming[:, :strata_mesh].T,
        incoming[:, strata_mesh:].T,
        sun_in[:, 0],
        sun_in[:, 1],
        cloudy_member_factors,
        arid_opacity_table,
        moisture_attenuation,
        blackbody_share,
        insolation_per_quadrature,
    )
    summed = lax.psum(partial_value, "grp")
    returning = lax.all_to_all(
        summed.T.reshape(tile_count, capacity, strata_mesh),
        "tile",
        split_axis=0,
        concat_axis=0,
        tiled=True,
    )
    total_heat = returning.reshape(slots, strata_mesh)[slot_index].T
    heating = (total_heat / NG).reshape(strata_mesh, parallel_band_sequence, meridian_boxes)
    return (heating, temp_dyn + heating, vapour_next)


def solution(mesh):
    in_specs = (
        P(None, "tile", None),
        P(None, "tile", None),
        P("tile", None),
        P("tile", None),
        P("tile", None),
        P("tile", None),
        P("grp", "tile"),
        P("grp", None),
        P("grp"),
        P("grp"),
        P("grp"),
    )
    out_specs = (P(None, "tile", None), P(None, "tile", None), P(None, "tile", None))
    return jax.shard_map(
        on_device, mesh=mesh, in_specs=in_specs, out_specs=out_specs, check_vma=False
    )
```

profile of v0, /device:TPU:1, one launch (start us, length us, event | category | flops | bytes accessed | tf_op | source)
XLA Modules:
  0.0 282.9 jit_solution(3957127956137913107)
XLA Ops:
  9.2 8.8 %collective-permute-start.1 = (f32[2,90,1,256]{1,3,2,0:T(8,128)S(1)}, f32[2,90,1,256]{1,3,2,0:T(8,128)S(1)}, u32[]{:S(2)}, u32[]{:S(2)}) collective-permute-start(f32[2,90,1,256]{1,3,2,0:T(8,128)S(1)} %pad_maximum_fusion), channel_id=1, source_target_pairs={{4,0},{8,4},{12,8},{16,12},{20,16},{24,20},{28,24},{32,28},{36,32}... | collective-permute-start | bytes 552968 | tf_op jit(solution)/shard_map/ppermute | solution.py:19
  18.0 1.9 collective-permute-start
  24.2 1.3 scatter_fusion
  25.5 1.5 copy.61
  27.0 12.7 %all-to-all-start.1 = ((f32[128,4,2]{1,2,0:T(2,128)}), f32[128,4,2]{1,2,0:T(2,128)S(1)}, u32[]{:S(2)}, u32[]{:S(2)}) async-start(f32[128,4,2]{1,2,0:T(2,128)} %copy.61), calls=%async_computation.1 | async-start | bytes 262144 | tf_op jit(solution)/shard_map/all_to_all | solution.py:147
  39.9 2.8 collective-permute-start.3
  42.7 2.8 collective-permute-start.2
  45.5 2.3 collective-permute-done.3
  48.9 1.7 scatter_custom_fusion
  52.4 15.6 %all-to-all-start = ((f32[128,4,180]{2,1,0:T(4,128)}), f32[128,4,180]{2,1,0:T(4,128)}, u32[]{:S(2)}, u32[]{:S(2)}) async-start(f32[128,4,180]{2,1,0:T(4,128)} %reshape.191), calls=%async_computation | async-start | bytes 1048576 | tf_op jit(solution)/shard_map/all_to_all | solution.py:146
  68.3 1.3 reshape.193
  69.7 1.3 reshape.194
  71.0 1.6 reshape.189
  74.2 14.0 %all-to-all-done = f32[128,4,180]{2,1,0:T(4,128)} async-done(((f32[128,4,180]{2,1,0:T(4,128)}), f32[128,4,180]{2,1,0:T(4,128)}, u32[]{:S(2)}, u32[]{:S(2)}) %all-to-all-start) | async-done | bytes 368672 | tf_op jit(solution)/shard_map/all_to_all | solution.py:146
  88.2 2.0 reshape.192
  90.2 2.0 slice_bitcast_fusion
  94.4 103.7 %while.12 = (s32[]{:T(128)}, f32[14,90,512]{2,1,0:T(8,128)S(1)}, f32[14,4,90]{2,1,0:T(4,128)}, f32[14,4]{1,0:T(8,128)S(1)}, f32[14,4,512]{2,1,0:T(4,128)}, /*ind...) while((s32[]{:T(128)}, f32[14,90,512]{2,1,0:T(8,128)S(1)}, ...), condition=%wide.region_7.8_spmd.clone.clone, body=%wide.region_5.7_spmd.clone.clone.sunk | while | flops 608476160 | bytes 12221821 | solution.py:79
  98.7 1.4 fusion.79
  100.2 1.5 fusion.81
  106.1 1.4 fusion.79
  107.6 1.5 fusion.81
  113.5 1.4 fusion.79
  115.0 1.5 fusion.81
  121.0 1.4 fusion.79
  122.4 1.5 fusion.81
  128.3 1.4 fusion.79
  129.8 1.5 fusion.81
  135.8 1.4 fusion.79
  137.2 1.5 fusion.81
  143.2 1.4 fusion.79
  144.6 1.5 fusion.81
  150.6 1.4 fusion.79
  152.0 1.5 fusion.81
  158.0 1.4 fusion.79
  159.4 1.5 fusion.81
  165.4 1.4 fusion.79
  166.8 1.5 fusion.81
  172.8 1.4 fusion.79
  174.2 1.5 fusion.81
  180.2 1.4 fusion.79
  181.6 1.5 fusion.81
  187.6 1.4 fusion.79
  189.0 1.5 fusion.81
  195.0 1.4 fusion.79
  196.4 1.5 fusion.81
  199.2 42.9 %all-reduce.2.cloned.1.call-done = f32[128,4,90]{2,1,0:T(4,128)} async-done(((f32[128,4,90]{2,1,0:T(4,128)}), f32[128,4,90]{2,1,0:T(4,128)}) %all-reduce.2.cloned.1.call-update) | async-done | bytes 184336 | tf_op jit(solution)/shard_map/psum | solution.py:162
  242.1 16.4 %all-to-all-start.2 = ((f32[128,4,90]{2,1,0:T(4,128)}), f32[128,4,90]{2,1,0:T(4,128)S(1)}, u32[]{:S(2)}, u32[]{:S(2)}) async-start(f32[128,4,90]{2,1,0:T(4,128)} %all-reduce.2.cloned.1.call-done), calls=%async_computation.2 | async-start | bytes 524288 | tf_op jit(solution)/shard_map/all_to_all | solution.py:163
  259.3 14.5 %all-to-all-done.2 = f32[128,4,90]{2,1,0:T(4,128)S(1)} async-done(((f32[128,4,90]{2,1,0:T(4,128)}), f32[128,4,90]{2,1,0:T(4,128)S(1)}, u32[]{:S(2)}, u32[]{:S(2)}) %all-to-all-start.2) | async-done | bytes 184352 | tf_op jit(solution)/shard_map/all_to_all | solution.py:163
  (249 shorter events, 78.8 us)
Async XLA Ops:
  7.2 17.0 %copy-start = (f32[512,2]{1,0:T(8,128)S(1)}, f32[512,2]{1,0:T(8,128)}, u32[]{:S(2)}) copy-start(f32[512,2]{1,0:T(8,128)} %constant.42.clone.1) | copy-start | bytes 12292
  9.2 30.5 %collective-permute-start.1 = (f32[2,90,1,256]{1,3,2,0:T(8,128)S(1)}, f32[2,90,1,256]{1,3,2,0:T(8,128)S(1)}, u32[]{:S(2)}, u32[]{:S(2)}) collective-permute-start(f32[2,90,1,256]{1,3,2,0:T(8,128)S(1)} %pad_maximum_fusion), channel_id=1, source_target_pairs={{4,0},{8,4},{12,8},{16,12},{20,16},{24,20},{28,24},{32,28},{36,32}... | collective-permute-start | bytes 552968 | tf_op jit(solution)/shard_map/ppermute | solution.py:19
  18.0 21.7 %collective-permute-start = (f32[2,90,1,256]{1,3,2,0:T(8,128)S(1)}, f32[2,90,1,256]{1,3,2,0:T(8,128)S(1)}, u32[]{:S(2)}, u32[]{:S(2)}) collective-permute-start(f32[2,90,1,256]{1,3,2,0:T(8,128)S(1)} %pad_maximum_fusion), channel_id=1, source_target_pairs={{0,4},{4,8},{8,12},{12,16},{16,20},{20,24},{24,28},{28,32},{32,36}... | collective-permute-start | bytes 552968 | tf_op jit(solution)/shard_map/ppermute | solution.py:16
  20.7 19.0 %copy-start.2 = (f32[1,256]{1,0:T(1,128)S(1)}, f32[1,256]{1,0:T(1,128)}, u32[]{:S(2)}) copy-start(f32[1,256]{1,0:T(1,128)} %param.15) | copy-start | bytes 3076
  27.0 25.5 %all-to-all-start.1 = ((f32[128,4,2]{1,2,0:T(2,128)}), f32[128,4,2]{1,2,0:T(2,128)S(1)}, u32[]{:S(2)}, u32[]{:S(2)}) async-start(f32[128,4,2]{1,2,0:T(2,128)} %copy.61), calls=%async_computation.1 | async-start | bytes 262144 | tf_op jit(solution)/shard_map/all_to_all | solution.py:147
  39.9 8.0 %collective-permute-start.3 = (f32[2,90,1,256]{1,3,2,0:T(8,128)S(1)}, f32[2,90,1,256]{1,3,2,0:T(8,128)S(1)}, u32[]{:S(2)}, u32[]{:S(2)}) collective-permute-start(f32[2,90,1,256]{1,3,2,0:T(8,128)S(1)} %fusion.45), channel_id=1, source_target_pairs={{4,0},{8,4},{12,8},{16,12},{20,16},{24,20},{28,24},{32,28},{36,32}... | collective-permute-start | bytes 552968 | tf_op jit(solution)/shard_map/ppermute | solution.py:19
  42.7 6.1 %collective-permute-start.2 = (f32[2,90,1,256]{1,3,2,0:T(8,128)S(1)}, f32[2,90,1,256]{1,3,2,0:T(8,128)S(1)}, u32[]{:S(2)}, u32[]{:S(2)}) collective-permute-start(f32[2,90,1,256]{1,3,2,0:T(8,128)S(1)} %fusion.45), channel_id=1, source_target_pairs={{0,4},{4,8},{8,12},{12,16},{16,20},{20,24},{24,28},{28,32},{32,36}... | collective-permute-start | bytes 552968 | tf_op jit(solution)/shard_map/ppermute | solution.py:16
  45.5 22.7 %copy-start.4 = (f32[56]{0:T(128)S(1)}, f32[56]{0:T(128)}, u32[]{:S(2)}) copy-start(f32[56]{0:T(128)} %param.21) | copy-start | bytes 676
  52.4 15.6 %copy-start.1 = (f32[128,4,2]{1,2,0:T(2,128)}, f32[128,4,2]{1,2,0:T(2,128)S(1)}, u32[]{:S(2)}) copy-start(f32[128,4,2]{1,2,0:T(2,128)S(1)} %all-to-all-done.1) | copy-start | bytes 12292
  52.4 35.8 %all-to-all-start = ((f32[128,4,180]{2,1,0:T(4,128)}), f32[128,4,180]{2,1,0:T(4,128)}, u32[]{:S(2)}, u32[]{:S(2)}) async-start(f32[128,4,180]{2,1,0:T(4,128)} %reshape.191), calls=%async_computation | async-start | bytes 1048576 | tf_op jit(solution)/shard_map/all_to_all | solution.py:146
  68.0 174.1 %all-reduce.2.cloned.1.call-start = ((), (), s32[]{:S(2)}) async-start(), calls=%async_computation.3 | async-start | bytes 524288 | tf_op jit(solution)/shard_map/psum | solution.py:162
  98.4 1.7 copy-start.3
  105.9 1.7 copy-start.3
  113.3 1.7 copy-start.3
  120.7 1.7 copy-start.3
  128.1 1.7 copy-start.3
  135.5 1.7 copy-start.3
  142.9 1.7 copy-start.3
  150.3 1.7 copy-start.3
  157.7 1.7 copy-start.3
  165.1 1.7 copy-start.3
  172.5 1.7 copy-start.3
  179.9 1.7 copy-start.3
  187.3 1.7 copy-start.3
  194.7 1.7 copy-start.3
  242.1 31.7 %all-to-all-start.2 = ((f32[128,4,90]{2,1,0:T(4,128)}), f32[128,4,90]{2,1,0:T(4,128)S(1)}, u32[]{:S(2)}, u32[]{:S(2)}) async-start(f32[128,4,90]{2,1,0:T(4,128)} %all-reduce.2.cloned.1.call-done), calls=%async_computation.2 | async-start | bytes 524288 | tf_op jit(solution)/shard_map/all_to_all | solution.py:163
Sparse Core Ops, SparseCore 0:
  199.4 42.6 all-reduce.1
where the time goes:
time: 286 us; the launch traced here: 283 us
  waiting for transfers between devices  75.5 us (26%)
  starting transfers between devices  61.2 us (21%)
  matrix products  54.1 us (19%)
  local copies, waits for them, and re-layouts  52.1 us (18%)
  other arithmetic  24.2 us (8%)
  between operations  14.3 us (5%)
    psum x1, waiting for transfers between devices, on_device(): summed = lax.psum(partial_value, 'grp')  42.9 us
    dot_general x14, matrix products, layer_pass(): jnp.einsum('lk,gkm->glm', lower_mask, infrared_radiance * growth[:, :stra...  21.2 us
    dot_general x14, matrix products, layer_pass(): jnp.einsum('lk,gkm->glm', upper_mask, infrared_radiance * damped[:, :stra...  19.8 us
    all_to_all x1, starting transfers between devices, on_device(): lax.all_to_all(summed.T.reshape(tile_count, capacity, strata_mesh), 'tile...  16.4 us
    all_to_all x1, starting transfers between devices, on_device(): lax.all_to_all(outgoing, 'tile', split_axis=0, concat_axis=0, tiled=True)  15.6 us
    all_to_all x1, waiting for transfers between devices, on_device(): lax.all_to_all(summed.T.reshape(tile_count, capacity, strata_mesh), 'tile...  14.5 us
    all_to_all x1, waiting for transfers between devices, on_device(): lax.all_to_all(outgoing, 'tile', split_axis=0, concat_axis=0, tiled=True)  14 us
    dot_general x14, matrix products, layer_pass(): jnp.einsum('lk,gkm->glm', lower_mask, thickness, precision=lax.Precision....  13.1 us
  transfers between devices with their start and end apart: 8, of which 6 were waited for; matrix products, arithmetic and copies ran while one was open for 6% of the time, Pallas kernels for 0%

commit v1 on v0

v1 whole, which is shorter than its diff:
```python
import functools
import math

import jax
import jax.numpy as jnp
from jax import lax
from jax.experimental import pallas as pl
from jax.experimental.pallas import tpu as pltpu
from jax.sharding import PartitionSpec as P

F32 = jnp.float32
CORES, ROWS_Y = 2, 8
CAP = 4
SLOT = 64
MESH = pl.DeviceIdType.MESH
LOG2E = math.log2(math.e)


def remote(src, dst, send, recv, where):
    return pltpu.make_async_remote_copy(
        src_ref=src, dst_ref=dst, send_sem=send, recv_sem=recv, device_id=where, device_id_type=MESH
    )


def fold8(x):
    parts = [x[8 * k : 8 * k + 8] for k in range(x.shape[0] // 8)]
    while len(parts) > 1:
        parts = [sum(parts[k : k + 2][1:], parts[k]) for k in range(0, len(parts), 2)]
    return parts[0]


def radiation_kernel(
    dims,
    kel, moi, spread, mu, lit, owner, fac, arid, matt, share, insol,
    heat_o, temp_o, vap_o,
    facv, fact, out1, mid, out2, got,
    t0, q0, t1, q1, t2, q2, halo1, halo2, dts,
    dry, tbuf, mbuf, acc, flux, gbuf, wbuf,
    load_sem, h1s, h1r, h2s, h2r, p1s, p1r, p2s, p2r, gs, gr,
):
    tiles, ydim, groups = dims
    zcdim = tiles // ydim
    levels = t0.shape[0]
    gpts = arid.shape[0]
    cols = t0.shape[1]
    me, grp = lax.axis_index("tile"), lax.axis_index("grp")
    core, y, z = lax.rem(me, CORES), lax.rem(me // CORES, ydim), me // (CORES * ydim)
    zc = z * CORES + core

    def at_zc(k):
        other = lax.rem(zc + k, zcdim)
        return (other // CORES) * (CORES * ydim) + y * CORES + lax.rem(other, CORES), other

    def at_y(k):
        other = lax.rem(y + k, ydim)
        return z * (CORES * ydim) + other * CORES + core, other

    south, north = lax.rem(me + 1, tiles), lax.rem(me + tiles - 1, tiles)

    peers = [{"tile": at_zc(k)[0]} for k in range(1, zcdim)]
    peers += [{"tile": at_y(k)[0]} for k in range(1, ydim)]
    peers += [{"grp": lax.rem(grp + k, groups)} for k in range(1, groups)]
    peers += [{"tile": south}, {"tile": north}]
    barrier = pltpu.get_barrier_semaphore()
    for peer in peers:
        pl.semaphore_signal(barrier, inc=1, device_id=peer, device_id_type=MESH)

    loads = [
        pltpu.make_async_copy(src, dst, load_sem.at[k])
        for k, (src, dst) in enumerate(((fac, facv), (kel.at[:, 0, :], t0), (moi.at[:, 0, :], q0)))
    ]
    for load in loads:
        load.start()

    loads[0].wait()
    tall = jnp.concatenate([facv[...], jnp.zeros((128 - gpts, facv.shape[1]), F32)], axis=0)
    fact[...] = tall.T
    step = CORES * CAP
    for other in range(zcdim):
        base = (other // CORES) * (ydim * step) + (other % CORES) * CAP
        rows = [fact[pl.ds(base + r, ydim, stride=step), :] for r in range(CAP)]
        for half in range(CAP // 2):
            out1[other, :, 128 * half : 128 * half + 128] = rows[2 * half] + pltpu.roll(
                rows[2 * half + 1], SLOT, 1
            )

    pl.semaphore_wait(barrier, len(peers))

    def halo(sources, buffers, send, recv):
        copies = []
        for field, source in enumerate(sources):
            for side, where in enumerate((south, north)):
                k = 2 * field + side
                copies.append(
                    remote(source, buffers.at[side, field], send.at[k], recv.at[k], {"tile": where})
                )
        for copy in copies:
            copy.start()
        return copies

    first = halo((kel.at[:, 0, :], moi.at[:, 0, :]), halo1, h1s, h1r)

    phase1 = []
    for k in range(1, zcdim):
        where, other = at_zc(k)
        phase1.append(
            remote(out1.at[other], mid.at[zc], p1s.at[k], p1r.at[k], {"tile": where})
        )
        phase1[-1].start()
    mid[zc] = out1[zc]

    own = owner[...]
    place = (lax.rem(own // CORES, ydim) * zcdim + (own // (CORES * ydim)) * CORES + lax.rem(own, CORES))
    hot = jnp.where(lax.broadcasted_iota(jnp.int32, (tiles, cols), 0) == place, 1.0, 0.0)
    before = jnp.where(
        lax.broadcasted_iota(jnp.int32, (cols, cols), 0) < lax.broadcasted_iota(jnp.int32, (cols, cols), 1),
        1.0,
        0.0,
    )
    earlier = jnp.dot(hot.astype(jnp.bfloat16), before.astype(jnp.bfloat16), preferred_element_type=F32)
    rank = jnp.sum(hot * earlier, axis=0, keepdims=True)

    for l in range(levels):
        dry[l] = jnp.broadcast_to(arid[:, l : l + 1] * (-LOG2E), (gpts, 128))

    def column(row):
        return jnp.broadcast_to(row[...], (128, gpts)).T

    share_c, insol_c, matt_c = column(share), column(insol), column(matt) * (-LOG2E)
    inv_mu = 1.0 / mu[...]
    sun = mu[...] * lit[...].astype(F32)

    coefficient = spread[...]

    def advance(x, far_north, far_south):
        n = jnp.where(me > 0, far_north, 0.0)
        s = jnp.where(me < tiles - 1, far_south, 0.0)
        east, west = pltpu.roll(x, cols - 1, 1), pltpu.roll(x, 1, 1)
        return x + coefficient * (n + s + east + west - 4.0 * x)

    loads[1].wait()
    loads[2].wait()
    for copy in first:
        copy.wait_recv()
    t1[...] = advance(t0[...], halo1[0, 0], halo1[1, 0])
    q1[...] = advance(q0[...], halo1[0, 1], halo1[1, 1])
    second = halo((t1, q1), halo2, h2s, h2r)

    for copy in phase1:
        copy.wait_recv()
    for other in range(ydim):
        for zz in range(zcdim):
            out2[other, zz : zz + 1, :] = mid[zz, other : other + 1, :]
    phase2 = []
    for k in range(1, ydim):
        where, other = at_y(k)
        phase2.append(remote(out2.at[other], got.at[y], p2s.at[k], p2r.at[k], {"tile": where}))
        phase2[-1].start()
    got[y] = out2[y]

    for copy in second:
        copy.wait_recv()
    t2[...] = advance(t1[...], halo2[0, 0], halo2[1, 0])
    vapour = advance(q1[...], halo2[0, 1], halo2[1, 1])
    temp_o[...] = t2[...]
    vap_o[...] = vapour
    q2[...] = vapour.reshape(levels, 1, cols)
    dts[0] = -t2[0:1, :]
    dts[1:levels] = (t2[0 : levels - 1, :] - t2[1:levels, :]).reshape(levels - 1, 1, cols)
    dts[levels] = t2[levels - 1 : levels, :]

    for copy in phase2:
        copy.wait_recv()
    table = got[...].reshape(tiles, CAP * SLOT)
    picked = lax.dot_general(
        table, hot, (((0,), (0,)), ((), ())), precision=lax.Precision.HIGHEST, preferred_element_type=F32
    )
    chosen = jnp.zeros((gpts, cols), F32)
    for r in range(CAP):
        chosen = jnp.where(rank == float(r), picked[r * SLOT : r * SLOT + gpts], chosen)
    for half in range(cols // 128):
        wbuf[half] = chosen[:, 128 * half : 128 * half + 128] * matt_c

    reduce = []
    for half in range(cols // 128):
        lanes = pl.ds(128 * half, 128)
        w = wbuf[half]
        inv = inv_mu[:, 128 * half : 128 * half + 128]
        s0 = insol_c * sun[:, 128 * half : 128 * half + 128]

        def down(l, carry, w=w, inv=inv, lanes=lanes):
            d, s = carry
            a = dry[l] + w * q2[l, :, lanes]
            t, u = jnp.exp2(a), jnp.exp2(a * inv)
            m = t * d
            tbuf[l] = t
            mbuf[l] = m
            s = s * u
            acc[l + 1] = fold8(s)
            return m + dts[l + 1, :, lanes], s

        def up(i, e, lanes=lanes):
            l = levels - 1 - i
            acc[l + 1] += fold8((mbuf[l] - e) * share_c)
            return tbuf[l] * e + dts_minus(l, lanes)

        def dts_minus(l, lanes):
            return -dts[l, :, lanes]

        start = jnp.broadcast_to(dts[0, :, lanes], (gpts, 128))
        lax.fori_loop(0, levels, down, (start, s0), unroll=2)
        e = lax.fori_loop(0, levels, up, jnp.zeros((gpts, 128), F32), unroll=2)
        acc[0] = fold8(s0 - share_c * e)
        total = acc[:, 0, :]
        for k in range(1, 8):
            total = total + acc[:, k, :]
        flux[...] = total
        gbuf[half, grp] = flux[0:levels, :] - flux[1 : levels + 1, :]
        for k in range(1, groups):
            reduce.append(
                remote(
                    gbuf.at[half, grp], gbuf.at[half, grp], gs.at[half, k], gr.at[half, k],
                    {"grp": lax.rem(grp + k, groups)},
                )
            )
            reduce[-1].start()

    for half in range(cols // 128):
        for copy in reduce[half * (groups - 1) : (half + 1) * (groups - 1)]:
            copy.wait_recv()
        total = gbuf[half, 0]
        for k in range(1, groups):
            total = total + gbuf[half, k]
        heat_o[:, 128 * half : 128 * half + 128] = total * (1.0 / (groups * gpts))
    for copy in first + second + phase1 + phase2 + reduce:
        copy.wait_send()


def on_device(
    tiles, ydim, groups,
    kelvin, moisture, spread, mu, lit, owner, fac, arid, matt, share, insol,
):
    levels, _, cols = kelvin.shape
    gpts, slots = fac.shape
    zcdim = tiles // ydim
    vmem, hbm = pl.BlockSpec(memory_space=pltpu.VMEM), pl.BlockSpec(memory_space=pl.ANY)
    dma = pltpu.SemaphoreType.DMA
    field = pltpu.VMEM((levels, cols), F32)
    out = jax.ShapeDtypeStruct((levels, cols), F32)
    heat, temp, vap = pl.pallas_call(
        functools.partial(radiation_kernel, (tiles, ydim, groups)),
        out_shape=(out, out, out),
        in_specs=[hbm, hbm, vmem, vmem, vmem, vmem, hbm, vmem, vmem, vmem, vmem],
        out_specs=(vmem, vmem, vmem),
        scratch_shapes=[
            pltpu.VMEM((gpts, slots), F32),
            pltpu.VMEM((slots, 128), F32),
            pltpu.VMEM((zcdim, ydim, CAP * SLOT), F32),
            pltpu.VMEM((zcdim, ydim, CAP * SLOT), F32),
            pltpu.VMEM((ydim, zcdim, CAP * SLOT), F32),
            pltpu.VMEM((ydim, zcdim, CAP * SLOT), F32),
            field, field, field, field, field,
            pltpu.VMEM((levels, 1, cols), F32),
            pltpu.VMEM((2, 2, levels, cols), F32),
            pltpu.VMEM((2, 2, levels, cols), F32),
            pltpu.VMEM((levels + 1, 1, cols), F32),
            pltpu.VMEM((levels, gpts, 128), F32),
            pltpu.VMEM((levels, gpts, 128), F32),
            pltpu.VMEM((levels, gpts, 128), F32),
            pltpu.VMEM((levels + 1, 8, 128), F32),
            pltpu.VMEM((levels + 1, 128), F32),
            pltpu.VMEM((cols // 128, groups, levels, 128), F32),
            pltpu.VMEM((cols // 128, gpts, 128), F32),
            dma((3,)), dma((4,)), dma((4,)), dma((4,)), dma((4,)),
            dma((zcdim,)), dma((zcdim,)), dma((ydim,)), dma((ydim,)),
            dma((2, groups)), dma((2, groups)),
        ],
        compiler_params=pltpu.CompilerParams(
            collective_id=0, has_side_effects=True, vmem_limit_bytes=40 * 2**20
        ),
    )(
        kelvin, moisture, spread, mu, lit, owner.reshape(1, cols), fac, arid,
        matt.reshape(1, gpts), share.reshape(1, gpts), insol.reshape(1, gpts),
    )
    heat, temp, vap = (x.reshape(kelvin.shape) for x in (heat, temp, vap))
    return heat, temp + heat, vap


def solution(mesh):
    tiles, groups = mesh.shape["tile"], mesh.shape["grp"]
    ydim = min(ROWS_Y, tiles // (2 * CORES))
    wide, row = P(None, "tile", None), P("tile", None)
    in_specs = (
        wide, wide, row, row, row, row, P("grp", "tile"), P("grp", None), P("grp"), P("grp"), P("grp"),
    )
    return jax.shard_map(
        functools.partial(on_device, tiles, ydim, groups),
        mesh=mesh,
        in_specs=in_specs,
        out_specs=(wide, wide, wide),
        check_vma=False,
    )
```

time: 286 us -> 45.5 us (0.16)
  the two profiles are of different devices: /device:TPU:1 before, /device:TPU:2 now
where the time goes in v1:
time: 45.5 us; the launch traced here: 45.2 us
  Pallas kernels  38.1 us (84%)
  local copies, waits for them, and re-layouts  6.33 us (14%)
  between operations  0.71 us (2%)
    pallas_call x1, Pallas kernels, on_device(): pl.pallas_call(functools.partial(radiation_kernel, (tiles, ydim, groups))...  38.1 us
    unnamed x25, local copies, waits for them, and re-layouts  6.33 us

profile of v1, /device:TPU:2, one launch (start us, length us, event | category | flops | bytes accessed | tf_op | source)
XLA Modules:
  0.0 45.2 jit_solution(8858506349353746868)
XLA Ops:
  0.6 0.0 copy-start.7
  0.6 0.0 copy-start.9
  0.7 0.0 copy-start.10
  0.7 0.0 copy-start.5
  0.7 0.0 copy-start.6
  0.7 0.0 copy-start.4
  0.7 0.0 copy-start.8
  0.7 0.6 %copy-done.7 = s32[256,1]{0,1:T(1,128)S(1)} copy-done((s32[256,1]{0,1:T(1,128)S(1)}, s32[256,1]{0,1:T(1,128)}, u32[]{:S(2)}) %copy-start.7) | copy-done | bytes 1048
  1.3 0.0 copy-done.9
  1.3 0.0 copy-done.10
  1.3 0.0 copy-done.5
  1.4 0.0 copy-done.6
  1.4 0.0 copy-done.4
  1.4 0.0 copy-done.8
  1.4 0.0 copy-start
  1.4 0.9 %copy-done = f32[56,512]{1,0:T(8,128)S(1)} copy-done((f32[56,512]{1,0:T(8,128)S(1)}, f32[56,512]{1,0:T(8,128)}, u32[]{:S(2)}) %copy-start) | copy-done | bytes 114712
  2.3 0.0 copy-start.1
  2.3 0.9 %copy-done.1 = f32[90,1,256]{2,1,0:T(1,128)S(1)} copy-done((f32[90,1,256]{2,1,0:T(1,128)S(1)}, f32[90,1,256]{2,1,0:T(1,128)}, u32[]{:S(2)}) %copy-start.1) | copy-done | bytes 92184
  3.2 0.0 copy-start.2
  3.2 0.9 %copy-done.2 = f32[90,1,256]{2,1,0:T(1,128)S(1)} copy-done((f32[90,1,256]{2,1,0:T(1,128)S(1)}, f32[90,1,256]{2,1,0:T(1,128)}, u32[]{:S(2)}) %copy-start.2) | copy-done | bytes 92184
  4.1 0.0 copy-start.3
  4.1 0.7 %copy-done.3 = f32[56,90]{1,0:T(8,128)S(1)} copy-done((f32[56,90]{1,0:T(8,128)S(1)}, f32[56,90]{1,0:T(8,128)}, u32[]{:S(2)}) %copy-start.3) | copy-done | bytes 20184
  4.8 38.1 %shard_map.130 = (f32[90,256]{1,0:T(8,128)S(1)}, f32[90,256]{1,0:T(8,128)S(1)}, f32[90,256]{1,0:T(8,128)S(1)}) custom-call(f32[90,1,256]{2,1,0:T(1,128)S(1)} %copy-done.1, f32[90,1,256]{2,1,0:T(1,128)S(1)} %copy-done.2, f32[1,256]{1,0:T(1,128)S(1)} %copy-done.4, f32[1,256]{1,0:T(1,128)S(1)} %copy-done.5, s32[1,256]{1,0:T(1,128)S(1)} %copy-done.6, ...), custom_call_target="tpu_custom_call" | custom-call | tf_op jit(solution)/shard_map/pallas_call | solution.py:250
  43.0 0.7 %copy.15 = f32[90,1,256]{2,1,0:T(1,128)} copy(f32[90,1,256]{2,0,1:T(8,128)S(1)} %add_bitcast_fusion) | data formatting | bytes 184320
  43.7 0.7 %copy.16 = f32[90,1,256]{2,1,0:T(1,128)} copy(f32[90,1,256]{2,0,1:T(8,128)S(1)} %bitcast.9) | data formatting | bytes 184320
  44.5 0.7 %copy.14 = f32[90,1,256]{2,1,0:T(1,128)} copy(f32[90,1,256]{2,0,1:T(8,128)S(1)} %bitcast.8) | data formatting | bytes 184320
  (1 shorter events, 0.0 us)
Async XLA Ops:
  0.6 0.7 %copy-start.7 = (s32[256,1]{0,1:T(1,128)S(1)}, s32[256,1]{0,1:T(1,128)}, u32[]{:S(2)}) copy-start(s32[256,1]{0,1:T(1,128)} %param.16) | copy-start | bytes 3076
  0.6 0.7 %copy-start.9 = (f32[56]{0:T(128)S(1)}, f32[56]{0:T(128)}, u32[]{:S(2)}) copy-start(f32[56]{0:T(128)} %param.20) | copy-start | bytes 676
  0.7 0.7 %copy-start.10 = (f32[56]{0:T(128)S(1)}, f32[56]{0:T(128)}, u32[]{:S(2)}) copy-start(f32[56]{0:T(128)} %param.21) | copy-start | bytes 676
  0.7 0.7 %copy-start.5 = (f32[1,256]{1,0:T(1,128)S(1)}, f32[1,256]{1,0:T(1,128)}, u32[]{:S(2)}) copy-start(f32[1,256]{1,0:T(1,128)} %mu.1) | copy-start | bytes 3076
  0.7 0.7 %copy-start.6 = (s32[1,256]{1,0:T(1,128)S(1)}, s32[1,256]{1,0:T(1,128)}, u32[]{:S(2)}) copy-start(s32[1,256]{1,0:T(1,128)} %lit.1) | copy-start | bytes 3076
  0.7 0.7 %copy-start.4 = (f32[1,256]{1,0:T(1,128)S(1)}, f32[1,256]{1,0:T(1,128)}, u32[]{:S(2)}) copy-start(f32[1,256]{1,0:T(1,128)} %spread.1) | copy-start | bytes 3076
  0.7 0.7 %copy-start.8 = (f32[56]{0:T(128)S(1)}, f32[56]{0:T(128)}, u32[]{:S(2)}) copy-start(f32[56]{0:T(128)} %param.19) | copy-start | bytes 676
  1.4 0.9 %copy-start = (f32[56,512]{1,0:T(8,128)S(1)}, f32[56,512]{1,0:T(8,128)}, u32[]{:S(2)}) copy-start(f32[56,512]{1,0:T(8,128)} %fac.1) | copy-start | bytes 344068
  2.3 0.9 %copy-start.1 = (f32[90,1,256]{2,1,0:T(1,128)S(1)}, f32[90,1,256]{2,1,0:T(1,128)}, u32[]{:S(2)}) copy-start(f32[90,1,256]{2,1,0:T(1,128)} %kel.1) | copy-start | bytes 276484
  3.2 0.9 %copy-start.2 = (f32[90,1,256]{2,1,0:T(1,128)S(1)}, f32[90,1,256]{2,1,0:T(1,128)}, u32[]{:S(2)}) copy-start(f32[90,1,256]{2,1,0:T(1,128)} %moi.1) | copy-start | bytes 276484
  4.1 0.7 %copy-start.3 = (f32[56,90]{1,0:T(8,128)S(1)}, f32[56,90]{1,0:T(8,128)}, u32[]{:S(2)}) copy-start(f32[56,90]{1,0:T(8,128)} %arid.1) | copy-start | bytes 60484

commit v2 on v1

--- a/solution.py
+++ b/solution.py
@@ -31,9 +31,9 @@
 
 def radiation_kernel(
     dims,
-    kel, moi, spread, mu, lit, owner, fac, arid, matt, share, insol,
+    kel, moi, spread_h, mu_h, lit_h, owner_h, fac, arid_h, matt_h, share_h, insol_h,
     heat_o, temp_o, vap_o,
-    facv, fact, out1, mid, out2, got,
+    facv, spread, mu, lit, owner, arid, matt, share, insol, fact, out1, mid, out2, got,
     t0, q0, t1, q1, t2, q2, halo1, halo2, dts,
     dry, tbuf, mbuf, acc, flux, gbuf, wbuf,
     load_sem, h1s, h1r, h2s, h2r, p1s, p1r, p2s, p2r, gs, gr,
@@ -67,7 +67,12 @@
 
     loads = [
         pltpu.make_async_copy(src, dst, load_sem.at[k])
-        for k, (src, dst) in enumerate(((fac, facv), (kel.at[:, 0, :], t0), (moi.at[:, 0, :], q0)))
+        for k, (src, dst) in enumerate(
+            (
+                (fac, facv), (kel.at[:, 0, :], t0), (moi.at[:, 0, :], q0), (owner_h, owner), (arid_h, arid),
+                (matt_h, matt), (share_h, share), (insol_h, insol), (mu_h, mu), (lit_h, lit), (spread_h, spread),
+            )
+        )
     ]
     for load in loads:
         load.start()
@@ -109,6 +114,8 @@
         phase1[-1].start()
     mid[zc] = out1[zc]
 
+    for load in loads[3:]:
+        load.wait()
     own = owner[...]
     place = (lax.rem(own // CORES, ydim) * zcdim + (own // (CORES * ydim)) * CORES + lax.rem(own, CORES))
     hot = jnp.where(lax.broadcasted_iota(jnp.int32, (tiles, cols), 0) == place, 1.0, 0.0)
@@ -208,8 +215,8 @@
             return -dts[l, :, lanes]
 
         start = jnp.broadcast_to(dts[0, :, lanes], (gpts, 128))
-        lax.fori_loop(0, levels, down, (start, s0), unroll=2)
-        e = lax.fori_loop(0, levels, up, jnp.zeros((gpts, 128), F32), unroll=2)
+        lax.fori_loop(0, levels, down, (start, s0), unroll=10)
+        e = lax.fori_loop(0, levels, up, jnp.zeros((gpts, 128), F32), unroll=10)
         acc[0] = fold8(s0 - share_c * e)
         total = acc[:, 0, :]
         for k in range(1, 8):
@@ -236,6 +243,22 @@
         copy.wait_send()
 
 
+def finish_kernel(heat, temp, vap, heat_o, temp_o, vap_o, heat_v, temp_v, vap_v, sem):
+    copies = []
+    for k, (value, buffer, out) in enumerate(
+        (
+            (vap[...], vap_v, vap_o),
+            (heat[...], heat_v, heat_o),
+            (temp[...] + heat[...], temp_v, temp_o),
+        )
+    ):
+        buffer[...] = value.reshape(buffer.shape)
+        copies.append(pltpu.make_async_copy(buffer, out, sem.at[k]))
+        copies[-1].start()
+    for copy in copies:
+        copy.wait()
+
+
 def on_device(
     tiles, ydim, groups,
     kelvin, moisture, spread, mu, lit, owner, fac, arid, matt, share, insol,
@@ -243,17 +266,19 @@
     levels, _, cols = kelvin.shape
     gpts, slots = fac.shape
     zcdim = tiles // ydim
-    vmem, hbm = pl.BlockSpec(memory_space=pltpu.VMEM), pl.BlockSpec(memory_space=pl.ANY)
+    vmem, hbm = pl.BlockSpec(memory_space=pltpu.VMEM), pl.BlockSpec(memory_space=pltpu.HBM)
     dma = pltpu.SemaphoreType.DMA
     field = pltpu.VMEM((levels, cols), F32)
     out = jax.ShapeDtypeStruct((levels, cols), F32)
     heat, temp, vap = pl.pallas_call(
         functools.partial(radiation_kernel, (tiles, ydim, groups)),
         out_shape=(out, out, out),
-        in_specs=[hbm, hbm, vmem, vmem, vmem, vmem, hbm, vmem, vmem, vmem, vmem],
+        in_specs=[hbm] * 11,
         out_specs=(vmem, vmem, vmem),
         scratch_shapes=[
             pltpu.VMEM((gpts, slots), F32),
+            pltpu.VMEM((1, cols), F32), pltpu.VMEM((1, cols), F32), pltpu.VMEM((1, cols), jnp.int32), pltpu.VMEM((1, cols), jnp.int32),
+            pltpu.VMEM((gpts, levels), F32), pltpu.VMEM((1, gpts), F32), pltpu.VMEM((1, gpts), F32), pltpu.VMEM((1, gpts), F32),
             pltpu.VMEM((slots, 128), F32),
             pltpu.VMEM((zcdim, ydim, CAP * SLOT), F32),
             pltpu.VMEM((zcdim, ydim, CAP * SLOT), F32),
@@ -271,19 +296,25 @@
             pltpu.VMEM((levels + 1, 128), F32),
             pltpu.VMEM((cols // 128, groups, levels, 128), F32),
             pltpu.VMEM((cols // 128, gpts, 128), F32),
-            dma((3,)), dma((4,)), dma((4,)), dma((4,)), dma((4,)),
+            dma((11,)), dma((4,)), dma((4,)), dma((4,)), dma((4,)),
             dma((zcdim,)), dma((zcdim,)), dma((ydim,)), dma((ydim,)),
             dma((2, groups)), dma((2, groups)),
         ],
         compiler_params=pltpu.CompilerParams(
-            collective_id=0, has_side_effects=True, vmem_limit_bytes=40 * 2**20
+            collective_id=0, has_side_effects=True, vmem_limit_bytes=56 * 2**20
         ),
     )(
         kelvin, moisture, spread, mu, lit, owner.reshape(1, cols), fac, arid,
         matt.reshape(1, gpts), share.reshape(1, gpts), insol.reshape(1, gpts),
     )
-    heat, temp, vap = (x.reshape(kelvin.shape) for x in (heat, temp, vap))
-    return heat, temp + heat, vap
+    out = jax.ShapeDtypeStruct(kelvin.shape, F32)
+    return pl.pallas_call(
+        finish_kernel,
+        out_shape=(out, out, out),
+        in_specs=[vmem] * 3,
+        out_specs=(hbm,) * 3,
+        scratch_shapes=[pltpu.VMEM(kelvin.shape, F32)] * 3 + [dma((3,))],
+    )(heat, temp, vap)
 
 
 def solution(mesh):

time: 45.5 us -> 40.4 us (0.89)
  local copies, waits for them, and re-layouts: 6.33 us -> 0 us
  Pallas kernels: 38.1 us -> 39.5 us
    unnamed x25 -> x0, local copies, waits for them, and re-layouts: 6.33 us -> none
    pallas_call x0 -> x1, Pallas kernels: none -> 1.74 us  [on_device(): pl.pallas_call(finish_kernel, out_shape=(out, out, out), in_specs=[vmem]...]
where the time goes in v2:
time: 40.4 us; the launch traced here: 40.2 us
  Pallas kernels  39.5 us (98%)
  between operations  0.64 us (2%)
    pallas_call x1, Pallas kernels, on_device(): pl.pallas_call(functools.partial(radiation_kernel, (tiles, ydim, groups))...  37.8 us
    pallas_call x1, Pallas kernels, on_device(): pl.pallas_call(finish_kernel, out_shape=(out, out, out), in_specs=[vmem]...  1.74 us

profile of v2, /device:TPU:2, one launch (start us, length us, event | category | flops | bytes accessed | tf_op | source)
XLA Modules:
  0.0 40.2 jit_solution(10554614067014514775)
XLA Ops:
  0.6 37.8 %shard_map.130 = (f32[90,256]{1,0:T(8,128)}, f32[90,256]{1,0:T(8,128)}, f32[90,256]{1,0:T(8,128)}) custom-call(f32[90,1,256]{2,1,0:T(1,128)} %kel.1, f32[90,1,256]{2,1,0:T(1,128)} %moi.1, f32[1,256]{1,0:T(1,128)} %spread_h.1, f32[1,256]{1,0:T(1,128)} %mu_h.1, s32[1,256]{1,0:T(1,128)} %lit_h.1, s32[1,256]{1,0:T(1,128)} %bitcast.4, f32[56,512]{1,0:T(8,128)} %fac.1, ...), custom_call_target="tpu_custom_call" | custom-call | tf_op jit(solution)/shard_map/pallas_call | solution.py:273
  38.4 1.7 %shard_map.131 = (f32[90,1,256]{2,1,0:T(1,128)}, f32[90,1,256]{2,1,0:T(1,128)}, f32[90,1,256]{2,1,0:T(1,128)}) custom-call(f32[90,256]{1,0:T(8,128)} %get-tuple-element.6.heat, f32[90,256]{1,0:T(8,128)} %get-tuple-element.7.temp, f32[90,256]{1,0:T(8,128)} %get-tuple-element.8.vap), custom_call_target="tpu_custom_call" | custom-call | tf_op jit(solution)/shard_map/pallas_call | solution.py:311

commit v3 on v2

v3 whole, which is shorter than its diff:
```python
import functools
import math

import jax
import jax.numpy as jnp
from jax import lax
from jax.experimental import pallas as pl
from jax.experimental.pallas import tpu as pltpu
from jax.sharding import PartitionSpec as P

F32 = jnp.float32
CORES, ROWS_Y = 2, 8
CAP = 4
SLOT = 64
MESH = pl.DeviceIdType.MESH
LOG2E = math.log2(math.e)


def remote(src, dst, send, recv, where):
    return pltpu.make_async_remote_copy(
        src_ref=src, dst_ref=dst, send_sem=send, recv_sem=recv, device_id=where, device_id_type=MESH
    )


def far_first(n):
    return sorted(range(n), key=lambda d: -min(d, n - d))


def pair(rows, base, count, step):
    low, high = (rows[pl.ds(base + r, count, stride=step), :] for r in (0, 1))
    return low + pltpu.roll(high, SLOT, 1)


def fold8(x):
    parts = [x[8 * k : 8 * k + 8] for k in range(x.shape[0] // 8)]
    while len(parts) > 1:
        parts = [sum(parts[k : k + 2][1:], parts[k]) for k in range(0, len(parts), 2)]
    return parts[0]


def radiation_kernel(
    dims,
    kel, moi, spread_h, mu_h, lit_h, owner_h, fac, arid_h, matt_h, share_h, insol_h,
    heat_o, temp_o, vap_o,
    facv, spread, mu, lit, owner, arid, matt, share, insol, fact, out1a, out1b, mida, midb, out2a, out2b, gota, gotb, hots,
    t0, q0, t1, q1, t2, q2, halo1, halo2, dts,
    dry, tbuf, mbuf, acc, flux, gbuf, wbuf,
    load_sem, h1s, h1r, h2s, h2r, p1s, p1r, p2s, p2r, gs, gr,
):
    tiles, ydim, groups = dims
    zcdim, ycdim = tiles // ydim, CORES * ydim
    levels = t0.shape[0]
    gpts = arid.shape[0]
    cols = t0.shape[1]
    me, grp = lax.axis_index("tile"), lax.axis_index("grp")
    core, y, z = lax.rem(me, CORES), lax.rem(me // CORES, ydim), me // (CORES * ydim)
    zdim = zcdim // CORES
    zc, yc = z * CORES + core, y * CORES + core

    def tile_of(a, b, c):
        return (a * ydim + b) * CORES + c

    near = [(d, c) for d in far_first(zdim) for c in (1, 0) if d or c]
    at_zc = []
    for d, c in near:
        zz, cc = lax.rem(z + d, zdim), lax.rem(core + c, CORES)
        at_zc.append((tile_of(zz, y, cc), zz * CORES + cc))
    at_yc = []
    for d, c in [(d, c) for d in far_first(ydim) for c in (1, 0) if d or c]:
        yy, cc = lax.rem(y + d, ydim), lax.rem(core + c, CORES)
        at_yc.append((tile_of(z, yy, cc), yy * CORES + cc))
    at_y = [(tile_of(z, lax.rem(y + d, ydim), core), lax.rem(y + d, ydim)) for d in far_first(ydim) if d]
    at_z = [(tile_of(lax.rem(z + d, zdim), y, core), lax.rem(z + d, zdim)) for d in far_first(zdim) if d]
    across = [k for k in far_first(groups) if k]

    south, north = lax.rem(me + 1, tiles), lax.rem(me + tiles - 1, tiles)

    peers = [{"tile": south}, {"tile": north}]
    peers += [{"tile": where} for where, _ in at_zc] + [{"tile": where} for where, _ in at_yc]
    peers += [{"grp": lax.rem(grp + k, groups)} for k in across]
    barrier = pltpu.get_barrier_semaphore()
    for peer in peers:
        pl.semaphore_signal(barrier, inc=1, device_id=peer, device_id_type=MESH)

    loads = [
        pltpu.make_async_copy(src, dst, load_sem.at[k])
        for k, (src, dst) in enumerate(
            (
                (fac, facv), (kel.at[:, 0, :], t0), (moi.at[:, 0, :], q0), (owner_h, owner), (arid_h, arid),
                (matt_h, matt), (share_h, share), (insol_h, insol), (mu_h, mu), (lit_h, lit), (spread_h, spread),
            )
        )
    ]
    for load in loads:
        load.start()

    loads[0].wait()
    tall = jnp.concatenate([facv[...], jnp.zeros((128 - gpts, facv.shape[1]), F32)], axis=0)
    fact[...] = tall.T
    step = CORES * CAP
    for k in range(zcdim):
        base = (k // CORES) * (ydim * step) + (k % CORES) * CAP
        out1a[k] = pair(fact, base, ydim, step)
    for k in range(ycdim):
        out1b[k] = pair(fact, k * CAP + 2, zdim, ydim * step)

    pl.semaphore_wait(barrier, len(peers))

    def halo(field, source, buffers, send, recv):
        copies = []
        for side, where in enumerate((south, north)):
            k = 2 * field + side
            copies.append(
                remote(source, buffers.at[side, field], send.at[k], recv.at[k], {"tile": where})
            )
            copies[-1].start()
        return copies

    first = [
        halo(field, source.at[:, 0, :], halo1, h1s, h1r) for field, source in enumerate((moi, kel))
    ]

    def spread_out(source, target, mine, partners, send, recv):
        copies = []
        for k, (where, other) in enumerate(partners):
            copies.append(
                remote(source.at[other], target.at[mine], send.at[k], recv.at[k], {"tile": where})
            )
            copies[-1].start()
        return copies

    phase1 = spread_out(out1a, mida, zc, at_zc, p1s.at[0], p1r.at[0])
    phase1 += spread_out(out1b, midb, yc, at_yc, p1s.at[1], p1r.at[1])
    mida[zc] = out1a[zc]
    midb[yc] = out1b[yc]

    for load in loads[3:]:
        load.wait()
    own = owner[...]
    place = lax.rem(own // CORES, ydim) * zcdim + (own // ycdim) * CORES + lax.rem(own, CORES)
    listed = lax.broadcasted_iota(jnp.int32, (tiles, cols), 0)
    hot = jnp.where(listed == own, 1.0, 0.0)
    before = jnp.where(
        lax.broadcasted_iota(jnp.int32, (cols, cols), 0) < lax.broadcasted_iota(jnp.int32, (cols, cols), 1),
        1.0,
        0.0,
    )
    earlier = jnp.dot(hot.astype(jnp.bfloat16), before.astype(jnp.bfloat16), preferred_element_type=F32)
    rank = jnp.sum(hot * earlier, axis=0, keepdims=True)
    hots[0:tiles] = jnp.where((listed == place) & (rank < 1.5), 1.0, 0.0).astype(jnp.bfloat16)
    hots[tiles : 2 * tiles] = jnp.where((listed == own) & (rank > 1.5), 1.0, 0.0).astype(jnp.bfloat16)
    odd = (rank == 1.0) | (rank == 3.0)

    for l in range(levels):
        dry[l] = jnp.broadcast_to(arid[:, l : l + 1] * (-LOG2E), (gpts, 128))

    def column(row):
        return jnp.broadcast_to(row[...], (128, gpts)).T

    share_c, insol_c, matt_c = column(share), column(insol), column(matt) * (-LOG2E)
    inv_mu = 1.0 / mu[...]
    sun = mu[...] * lit[...].astype(F32)

    coefficient = spread[...]

    def advance(x, far_north, far_south):
        n = jnp.where(me > 0, far_north, 0.0)
        s = jnp.where(me < tiles - 1, far_south, 0.0)
        east, west = pltpu.roll(x, cols - 1, 1), pltpu.roll(x, 1, 1)
        return x + coefficient * (n + s + east + west - 4.0 * x)

    loads[1].wait()
    loads[2].wait()

    def arrive(copies):
        for copy in copies:
            copy.wait_recv()

    arrive(first[0])
    q1[...] = advance(q0[...], halo1[0, 0], halo1[1, 0])
    second = [halo(0, q1, halo2, h2s, h2r)]
    arrive(first[1])
    t1[...] = advance(t0[...], halo1[0, 1], halo1[1, 1])
    second.append(halo(1, t1, halo2, h2s, h2r))

    arrive(phase1)
    for k in range(ydim):
        out2a[k] = mida.reshape(tiles, 2 * SLOT)[pl.ds(k, zcdim, stride=ydim), :]
    for k in range(zdim):
        out2b[k] = midb.reshape(tiles, 2 * SLOT)[pl.ds(k, ycdim, stride=zdim), :]
    phase2 = spread_out(out2a, gota, y, at_y, p2s.at[0], p2r.at[0])
    phase2 += spread_out(out2b, gotb, z, at_z, p2s.at[1], p2r.at[1])
    gota[y] = out2a[y]
    gotb[z] = out2b[z]

    arrive(second[0])
    vapour = advance(q1[...], halo2[0, 0], halo2[1, 0]).reshape(levels, 1, cols)
    q2[...] = vapour
    vap_o[...] = vapour
    arrive(second[1])
    t2[...] = advance(t1[...], halo2[0, 1], halo2[1, 1])
    dts[0] = -t2[0:1, :]
    dts[1:levels] = (t2[0 : levels - 1, :] - t2[1:levels, :]).reshape(levels - 1, 1, cols)
    dts[levels] = t2[levels - 1 : levels, :]

    arrive(phase2)
    table = jnp.concatenate(
        [gota[...].reshape(tiles, 2 * SLOT), gotb[...].reshape(tiles, 2 * SLOT)], axis=0
    )
    picked = jnp.zeros((2 * SLOT, cols), F32)
    for _ in range(3):
        part = table.astype(jnp.bfloat16)
        table = table - part.astype(F32)
        picked = picked + lax.dot_general(
            part, hots[...], (((0,), (0,)), ((), ())), preferred_element_type=F32
        )
    chosen = jnp.where(odd, picked[SLOT : SLOT + gpts], picked[0:gpts])
    for half in range(cols // 128):
        wbuf[half] = chosen[:, 128 * half : 128 * half + 128] * matt_c

    reduce = []
    for half in range(cols // 128):
        lanes = pl.ds(128 * half, 128)
        w = wbuf[half]
        inv = inv_mu[:, 128 * half : 128 * half + 128]
        s0 = insol_c * sun[:, 128 * half : 128 * half + 128]

        def down(l, carry, w=w, inv=inv, lanes=lanes):
            d, s = carry
            a = dry[l] + w * q2[l, :, lanes]
            t, u = jnp.exp2(a), jnp.exp2(a * inv)
            m = t * d
            tbuf[l] = t
            mbuf[l] = m
            s = s * u
            acc[l + 1] = fold8(s)
            return m + dts[l + 1, :, lanes], s

        def up(i, e, lanes=lanes):
            l = levels - 1 - i
            acc[l + 1] += fold8((mbuf[l] - e) * share_c)
            return tbuf[l] * e + dts_minus(l, lanes)

        def dts_minus(l, lanes):
            return -dts[l, :, lanes]

        start = jnp.broadcast_to(dts[0, :, lanes], (gpts, 128))
        lax.fori_loop(0, levels, down, (start, s0), unroll=10)
        e = lax.fori_loop(0, levels, up, jnp.zeros((gpts, 128), F32), unroll=10)
        acc[0] = fold8(s0 - share_c * e)
        total = acc[:, 0, :]
        for k in range(1, 8):
            total = total + acc[:, k, :]
        flux[...] = total
        gbuf[half, grp] = flux[0:levels, :] - flux[1 : levels + 1, :]
        for k in across:
            reduce.append(
                remote(
                    gbuf.at[half, grp], gbuf.at[half, grp], gs.at[half, k], gr.at[half, k],
                    {"grp": lax.rem(grp + k, groups)},
                )
            )
            reduce[-1].start()

    for half in range(cols // 128):
        for copy in reduce[half * (groups - 1) : (half + 1) * (groups - 1)]:
            copy.wait_recv()
        total = gbuf[half, 0]
        for k in range(1, groups):
            total = total + gbuf[half, k]
        lanes = pl.ds(128 * half, 128)
        total = total * (1.0 / (groups * gpts))
        heat_o[:, :, lanes] = total.reshape(levels, 1, 128)
        temp_o[:, :, lanes] = (t2[:, lanes] + total).reshape(levels, 1, 128)
    for copy in first[0] + first[1] + second[0] + second[1] + phase1 + phase2 + reduce:
        copy.wait_send()


def finish_kernel(heat, temp, vap, heat_o, temp_o, vap_o, sem):
    copies = [
        pltpu.make_async_copy(value, out, sem.at[k])
        for k, (value, out) in enumerate(((heat, heat_o), (temp, temp_o), (vap, vap_o)))
    ]
    for copy in copies:
        copy.start()
    for copy in copies:
        copy.wait()


def on_device(
    tiles, ydim, groups,
    kelvin, moisture, spread, mu, lit, owner, fac, arid, matt, share, insol,
):
    levels, _, cols = kelvin.shape
    gpts, slots = fac.shape
    zcdim, ycdim = tiles // ydim, CORES * ydim
    zdim = zcdim // CORES
    most = max(zcdim, ycdim)
    vmem, hbm = pl.BlockSpec(memory_space=pltpu.VMEM), pl.BlockSpec(memory_space=pltpu.HBM)
    dma = pltpu.SemaphoreType.DMA
    field = pltpu.VMEM((levels, cols), F32)
    out = pltpu.VMEM((levels, 1, cols), F32)
    heat, temp, vap = pl.pallas_call(
        functools.partial(radiation_kernel, (tiles, ydim, groups)),
        out_shape=(out, out, out),
        in_specs=[hbm] * 11,
        out_specs=(vmem, vmem, vmem),
        scratch_shapes=[
            pltpu.VMEM((gpts, slots), F32),
            pltpu.VMEM((1, cols), F32), pltpu.VMEM((1, cols), F32), pltpu.VMEM((1, cols), jnp.int32), pltpu.VMEM((1, cols), jnp.int32),
            pltpu.VMEM((gpts, levels), F32), pltpu.VMEM((1, gpts), F32), pltpu.VMEM((1, gpts), F32), pltpu.VMEM((1, gpts), F32),
            pltpu.VMEM((slots, 128), F32),
            pltpu.VMEM((zcdim, ydim, 128), F32), pltpu.VMEM((ycdim, zdim, 128), F32),
            pltpu.VMEM((zcdim, ydim, 128), F32), pltpu.VMEM((ycdim, zdim, 128), F32),
            pltpu.VMEM((ydim, zcdim, 128), F32), pltpu.VMEM((zdim, ycdim, 128), F32),
            pltpu.VMEM((ydim, zcdim, 128), F32), pltpu.VMEM((zdim, ycdim, 128), F32),
            pltpu.VMEM((2 * tiles, cols), jnp.bfloat16),
            field, field, field, field, field,
            pltpu.VMEM((levels, 1, cols), F32),
            pltpu.VMEM((2, 2, levels, cols), F32),
            pltpu.VMEM((2, 2, levels, cols), F32),
            pltpu.VMEM((levels + 1, 1, cols), F32),
            pltpu.VMEM((levels, gpts, 128), F32),
            pltpu.VMEM((levels, gpts, 128), F32),
            pltpu.VMEM((levels, gpts, 128), F32),
            pltpu.VMEM((levels + 1, 8, 128), F32),
            pltpu.VMEM((levels + 1, 128), F32),
            pltpu.VMEM((cols // 128, groups, levels, 128), F32),
            pltpu.VMEM((cols // 128, gpts, 128), F32),
            dma((11,)), dma((4,)), dma((4,)), dma((4,)), dma((4,)),
            dma((2, most)), dma((2, most)), dma((2, most)), dma((2, most)),
            dma((2, groups)), dma((2, groups)),
        ],
        compiler_params=pltpu.CompilerParams(
            collective_id=0, has_side_effects=True, vmem_limit_bytes=56 * 2**20
        ),
    )(
        kelvin, moisture, spread, mu, lit, owner.reshape(1, cols), fac, arid,
        matt.reshape(1, gpts), share.reshape(1, gpts), insol.reshape(1, gpts),
    )
    out = jax.ShapeDtypeStruct(kelvin.shape, F32)
    return pl.pallas_call(
        finish_kernel,
        out_shape=(out, out, out),
        in_specs=[vmem] * 3,
        out_specs=(hbm,) * 3,
        scratch_shapes=[dma((3,))],
        compiler_params=pltpu.CompilerParams(vmem_limit_bytes=2**20),
    )(heat, temp, vap)


def solution(mesh):
    tiles, groups = mesh.shape["tile"], mesh.shape["grp"]
    ydim = min(ROWS_Y, tiles // (2 * CORES))
    wide, row = P(None, "tile", None), P("tile", None)
    in_specs = (
        wide, wide, row, row, row, row, P("grp", "tile"), P("grp", None), P("grp"), P("grp"), P("grp"),
    )
    return jax.shard_map(
        functools.partial(on_device, tiles, ydim, groups),
        mesh=mesh,
        in_specs=in_specs,
        out_specs=(wide, wide, wide),
        check_vma=False,
    )
```

time: 40.4 us -> 38.1 us (0.943)
  the two profiles are of different devices: /device:TPU:2 before, /device:TPU:1 now
where the time goes in v3:
time: 38.1 us; the launch traced here: 38 us
  Pallas kernels  37.3 us (98%)
  between operations  0.64 us (2%)
    pallas_call x1, Pallas kernels, on_device(): pl.pallas_call(functools.partial(radiation_kernel, (tiles, ydim, groups))...  36.6 us

profile of v3, /device:TPU:1, one launch (start us, length us, event | category | flops | bytes accessed | tf_op | source)
XLA Modules:
  0.0 38.0 jit_solution(8170716182895899063)
XLA Ops:
  0.6 36.6 %shard_map.130 = (f32[90,1,256]{2,1,0:T(1,128)S(1)}, f32[90,1,256]{2,1,0:T(1,128)S(1)}, f32[90,1,256]{2,1,0:T(1,128)S(1)}) custom-call(f32[90,1,256]{2,1,0:T(1,128)} %kel.1, f32[90,1,256]{2,1,0:T(1,128)} %moi.1, f32[1,256]{1,0:T(1,128)} %spread_h.1, f32[1,256]{1,0:T(1,128)} %mu_h.1, s32[1,256]{1,0:T(1,128)} %lit_h.1, s32[1,256]{1,0:T(1,128)} %bitcast.4, ...), custom_call_target="tpu_custom_call" | custom-call | tf_op jit(solution)/shard_map/pallas_call | solution.py:303
  37.2 0.7 %shard_map.131 = (f32[90,1,256]{2,1,0:T(1,128)}, f32[90,1,256]{2,1,0:T(1,128)}, f32[90,1,256]{2,1,0:T(1,128)}) custom-call(f32[90,1,256]{2,1,0:T(1,128)S(1)} %get-tuple-element.6.heat, f32[90,1,256]{2,1,0:T(1,128)S(1)} %get-tuple-element.7.temp, f32[90,1,256]{2,1,0:T(1,128)S(1)} %get-tuple-element.8.vap), custom_call_target="tpu_custom_call" | custom-call | tf_op jit(solution)/shard_map/pallas_call | solution.py:342

commit v4 on v3

--- a/solution.py
+++ b/solution.py
@@ -43,15 +43,16 @@
     kel, moi, spread_h, mu_h, lit_h, owner_h, fac, arid_h, matt_h, share_h, insol_h,
     heat_o, temp_o, vap_o,
     facv, spread, mu, lit, owner, arid, matt, share, insol, fact, out1a, out1b, mida, midb, out2a, out2b, gota, gotb, hots,
-    t0, q0, t1, q1, t2, q2, halo1, halo2, dts,
+    mine, halo, coefs, q2, t2, dts,
     dry, tbuf, mbuf, acc, flux, gbuf, wbuf,
-    load_sem, h1s, h1r, h2s, h2r, p1s, p1r, p2s, p2r, gs, gr,
+    load_sem, hs, hr, cs, cr, xs, xr, vap_sem, p1s, p1r, p2s, p2r, gs, gr,
 ):
     tiles, ydim, groups = dims
     zcdim, ycdim = tiles // ydim, CORES * ydim
-    levels = t0.shape[0]
+    levels, _, cols = kel.shape
+    part = halo.shape[2]
+    gap = groups * part - levels
     gpts = arid.shape[0]
-    cols = t0.shape[1]
     me, grp = lax.axis_index("tile"), lax.axis_index("grp")
     core, y, z = lax.rem(me, CORES), lax.rem(me // CORES, ydim), me // (CORES * ydim)
     zdim = zcdim // CORES
@@ -73,9 +74,10 @@
     at_z = [(tile_of(lax.rem(z + d, zdim), y, core), lax.rem(z + d, zdim)) for d in far_first(zdim) if d]
     across = [k for k in far_first(groups) if k]
 
-    south, north = lax.rem(me + 1, tiles), lax.rem(me + tiles - 1, tiles)
-
-    peers = [{"tile": south}, {"tile": north}]
+    rows = [(lax.rem(me + tiles - d, tiles), k) for k, d in enumerate((-2, -1, 1, 2))]
+    level = jnp.minimum(grp * part, levels - part)
+
+    peers = [{"tile": where} for where, _ in rows]
     peers += [{"tile": where} for where, _ in at_zc] + [{"tile": where} for where, _ in at_yc]
     peers += [{"grp": lax.rem(grp + k, groups)} for k in across]
     barrier = pltpu.get_barrier_semaphore()
@@ -86,8 +88,9 @@
         pltpu.make_async_copy(src, dst, load_sem.at[k])
         for k, (src, dst) in enumerate(
             (
-                (fac, facv), (kel.at[:, 0, :], t0), (moi.at[:, 0, :], q0), (owner_h, owner), (arid_h, arid),
-                (matt_h, matt), (share_h, share), (insol_h, insol), (mu_h, mu), (lit_h, lit), (spread_h, spread),
+                (fac, facv), (moi.at[pl.ds(level, part), 0, :], mine.at[0]), (kel.at[pl.ds(level, part), 0, :], mine.at[1]),
+                (owner_h, owner), (arid_h, arid), (matt_h, matt), (share_h, share), (insol_h, insol), (mu_h, mu),
+                (lit_h, lit), (spread_h, spread),
             )
         )
     ]
@@ -106,19 +109,19 @@
 
     pl.semaphore_wait(barrier, len(peers))
 
-    def halo(field, source, buffers, send, recv):
-        copies = []
-        for side, where in enumerate((south, north)):
-            k = 2 * field + side
-            copies.append(
-                remote(source, buffers.at[side, field], send.at[k], recv.at[k], {"tile": where})
-            )
-            copies[-1].start()
-        return copies
-
-    first = [
-        halo(field, source.at[:, 0, :], halo1, h1s, h1r) for field, source in enumerate((moi, kel))
-    ]
+    halos = []
+    for where, k in rows:
+        for field, source in enumerate((moi, kel)):
+            halos.append(
+                remote(
+                    source.at[pl.ds(level, part), 0, :], halo.at[k, field], hs.at[k, field], hr.at[k, field],
+                    {"tile": where},
+                )
+            )
+        if k in (1, 2):
+            halos.append(remote(spread_h, coefs.at[k - 1], cs.at[k - 1], cr.at[k - 1], {"tile": where}))
+    for copy in halos:
+        copy.start()
 
     def spread_out(source, target, mine, partners, send, recv):
         copies = []
@@ -161,27 +164,31 @@
     inv_mu = 1.0 / mu[...]
     sun = mu[...] * lit[...].astype(F32)
 
-    coefficient = spread[...]
-
-    def advance(x, far_north, far_south):
-        n = jnp.where(me > 0, far_north, 0.0)
-        s = jnp.where(me < tiles - 1, far_south, 0.0)
+    def advance(x, coefficient, n, s):
         east, west = pltpu.roll(x, cols - 1, 1), pltpu.roll(x, 1, 1)
         return x + coefficient * (n + s + east + west - 4.0 * x)
-
-    loads[1].wait()
-    loads[2].wait()
 
     def arrive(copies):
         for copy in copies:
             copy.wait_recv()
 
-    arrive(first[0])
-    q1[...] = advance(q0[...], halo1[0, 0], halo1[1, 0])
-    second = [halo(0, q1, halo2, h2s, h2r)]
-    arrive(first[1])
-    t1[...] = advance(t0[...], halo1[0, 1], halo1[1, 1])
-    second.append(halo(1, t1, halo2, h2s, h2r))
+    loads[1].wait()
+    loads[2].wait()
+    arrive(halos)
+    shared = []
+    for field, whole in enumerate((q2, t2)):
+        x = [halo[0, field], halo[1, field], mine[field], halo[2, field], halo[3, field]]
+        x = [jnp.where((me + d >= 0) & (me + d < tiles), v, 0.0) for d, v in zip(range(-2, 3), x)]
+        north = jnp.where(me > 0, advance(x[1], coefs[0], x[0], x[2]), 0.0)
+        south = jnp.where(me < tiles - 1, advance(x[3], coefs[1], x[2], x[4]), 0.0)
+        own_row = advance(x[2], spread[...], x[1], x[3])
+        here = whole.at[pl.ds(grp * part, part)]
+        here[...] = advance(own_row, spread[...], north, south).reshape(part, 1, cols)
+        for k in across:
+            shared.append(
+                remote(here, here, xs.at[field, k], xr.at[field, k], {"grp": lax.rem(grp + k, groups)})
+            )
+            shared[-1].start()
 
     arrive(phase1)
     for k in range(ydim):
@@ -193,15 +200,21 @@
     gota[y] = out2a[y]
     gotb[z] = out2b[z]
 
-    arrive(second[0])
-    vapour = advance(q1[...], halo2[0, 0], halo2[1, 0]).reshape(levels, 1, cols)
-    q2[...] = vapour
-    vap_o[...] = vapour
-    arrive(second[1])
-    t2[...] = advance(t1[...], halo2[0, 1], halo2[1, 1])
-    dts[0] = -t2[0:1, :]
-    dts[1:levels] = (t2[0 : levels - 1, :] - t2[1:levels, :]).reshape(levels - 1, 1, cols)
-    dts[levels] = t2[levels - 1 : levels, :]
+    arrive(shared)
+    last = (groups - 1) * part
+    vapour = [
+        pltpu.make_async_copy(q2.at[pl.ds(0, last)], vap_o.at[pl.ds(0, last)], vap_sem.at[0]),
+        pltpu.make_async_copy(
+            q2.at[pl.ds(last + gap, levels - last)], vap_o.at[pl.ds(last, levels - last)], vap_sem.at[1]
+        ),
+    ]
+    for copy in vapour:
+        copy.start()
+    dts[0] = -t2[0]
+    dts[1:last] = t2[0 : last - 1] - t2[1:last]
+    dts[last] = t2[last - 1] - t2[last + gap]
+    dts[last + 1 : levels] = t2[last + gap : levels + gap - 1] - t2[last + gap + 1 : levels + gap]
+    dts[levels] = t2[levels + gap - 1]
 
     arrive(phase2)
     table = jnp.concatenate(
@@ -227,7 +240,7 @@
 
         def down(l, carry, w=w, inv=inv, lanes=lanes):
             d, s = carry
-            a = dry[l] + w * q2[l, :, lanes]
+            a = dry[l] + w * q2[jnp.where(l < last, l, l + gap), :, lanes]
             t, u = jnp.exp2(a), jnp.exp2(a * inv)
             m = t * d
             tbuf[l] = t
@@ -270,9 +283,13 @@
             total = total + gbuf[half, k]
         lanes = pl.ds(128 * half, 128)
         total = total * (1.0 / (groups * gpts))
-        heat_o[:, :, lanes] = total.reshape(levels, 1, 128)
-        temp_o[:, :, lanes] = (t2[:, lanes] + total).reshape(levels, 1, 128)
-    for copy in first[0] + first[1] + second[0] + second[1] + phase1 + phase2 + reduce:
+        total = total.reshape(levels, 1, 128)
+        heat_o[:, :, lanes] = total
+        temp_o[0:last, :, lanes] = t2[0:last, :, lanes] + total[0:last]
+        temp_o[last:levels, :, lanes] = t2[last + gap : levels + gap, :, lanes] + total[last:levels]
+    for copy in vapour:
+        copy.wait()
+    for copy in halos + shared + phase1 + phase2 + reduce:
         copy.wait_send()
 
 
@@ -298,7 +315,8 @@
     most = max(zcdim, ycdim)
     vmem, hbm = pl.BlockSpec(memory_space=pltpu.VMEM), pl.BlockSpec(memory_space=pltpu.HBM)
     dma = pltpu.SemaphoreType.DMA
-    field = pltpu.VMEM((levels, cols), F32)
+    part = -(-levels // (8 * groups)) * 8
+    whole = pltpu.VMEM((groups * part, 1, cols), F32)
     out = pltpu.VMEM((levels, 1, cols), F32)
     heat, temp, vap = pl.pallas_call(
         functools.partial(radiation_kernel, (tiles, ydim, groups)),
@@ -315,10 +333,10 @@
             pltpu.VMEM((ydim, zcdim, 128), F32), pltpu.VMEM((zdim, ycdim, 128), F32),
             pltpu.VMEM((ydim, zcdim, 128), F32), pltpu.VMEM((zdim, ycdim, 128), F32),
             pltpu.VMEM((2 * tiles, cols), jnp.bfloat16),
-            field, field, field, field, field,
-            pltpu.VMEM((levels, 1, cols), F32),
-            pltpu.VMEM((2, 2, levels, cols), F32),
-            pltpu.VMEM((2, 2, levels, cols), F32),
+            pltpu.VMEM((2, part, cols), F32),
+            pltpu.VMEM((4, 2, part, cols), F32),
+            pltpu.VMEM((2, 1, cols), F32),
+            whole, whole,
             pltpu.VMEM((levels + 1, 1, cols), F32),
             pltpu.VMEM((levels, gpts, 128), F32),
             pltpu.VMEM((levels, gpts, 128), F32),
@@ -327,7 +345,7 @@
             pltpu.VMEM((levels + 1, 128), F32),
             pltpu.VMEM((cols // 128, groups, levels, 128), F32),
             pltpu.VMEM((cols // 128, gpts, 128), F32),
-            dma((11,)), dma((4,)), dma((4,)), dma((4,)), dma((4,)),
+            dma((11,)), dma((4, 2)), dma((4, 2)), dma((2,)), dma((2,)), dma((2, groups)), dma((2, groups)), dma((2,)),
             dma((2, most)), dma((2, most)), dma((2, most)), dma((2, most)),
             dma((2, groups)), dma((2, groups)),
         ],

time: 38.1 us -> 37.3 us (0.979)
  Pallas kernels: 37.3 us -> 36.5 us
    pallas_call x1, Pallas kernels: 36.6 us -> 35.8 us  [on_device(): pl.pallas_call(functools.partial(radiation_kernel, (tiles, ydim, groups))...]
where the time goes in v4:
time: 37.3 us; the launch traced here: 37.1 us
  Pallas kernels  36.5 us (98%)
  between operations  0.64 us (2%)
    pallas_call x1, Pallas kernels, on_device(): pl.pallas_call(functools.partial(radiation_kernel, (tiles, ydim, groups))...  35.8 us

profile of v4, /device:TPU:1, one launch (start us, length us, event | category | flops | bytes accessed | tf_op | source)
XLA Modules:
  0.0 37.1 jit_solution(5867770945385275691)
XLA Ops:
  0.6 35.8 %shard_map.130 = (f32[90,1,256]{2,1,0:T(1,128)S(1)}, f32[90,1,256]{2,1,0:T(1,128)S(1)}, f32[90,1,256]{2,1,0:T(1,128)S(1)}) custom-call(f32[90,1,256]{2,1,0:T(1,128)} %kel.1, f32[90,1,256]{2,1,0:T(1,128)} %moi.1, f32[1,256]{1,0:T(1,128)} %spread_h.1, f32[1,256]{1,0:T(1,128)} %mu_h.1, s32[1,256]{1,0:T(1,128)} %lit_h.1, s32[1,256]{1,0:T(1,128)} %bitcast.4, ...), custom_call_target="tpu_custom_call" | custom-call | tf_op jit(solution)/shard_map/pallas_call | solution.py:321
  36.4 0.7 %shard_map.131 = (f32[90,1,256]{2,1,0:T(1,128)}, f32[90,1,256]{2,1,0:T(1,128)}, f32[90,1,256]{2,1,0:T(1,128)}) custom-call(f32[90,1,256]{2,1,0:T(1,128)S(1)} %get-tuple-element.6.heat, f32[90,1,256]{2,1,0:T(1,128)S(1)} %get-tuple-element.7.temp, f32[90,1,256]{2,1,0:T(1,128)S(1)} %get-tuple-element.8.vap), custom_call_target="tpu_custom_call" | custom-call | tf_op jit(solution)/shard_map/pallas_call | solution.py:360

commit v5 on v4

--- a/solution.py
+++ b/solution.py
@@ -80,10 +80,6 @@
     peers = [{"tile": where} for where, _ in rows]
     peers += [{"tile": where} for where, _ in at_zc] + [{"tile": where} for where, _ in at_yc]
     peers += [{"grp": lax.rem(grp + k, groups)} for k in across]
-    barrier = pltpu.get_barrier_semaphore()
-    for peer in peers:
-        pl.semaphore_signal(barrier, inc=1, device_id=peer, device_id_type=MESH)
-
     loads = [
         pltpu.make_async_copy(src, dst, load_sem.at[k])
         for k, (src, dst) in enumerate(
@@ -96,6 +92,10 @@
     ]
     for load in loads:
         load.start()
+
+    barrier = pltpu.get_barrier_semaphore()
+    for peer in peers:
+        pl.semaphore_signal(barrier, inc=1, device_id=peer, device_id_type=MESH)
 
     loads[0].wait()
     tall = jnp.concatenate([facv[...], jnp.zeros((128 - gpts, facv.shape[1]), F32)], axis=0)
@@ -109,6 +109,17 @@
 
     pl.semaphore_wait(barrier, len(peers))
 
+    def spread_out(source, target, mine, partners, send, recv):
+        copies = []
+        for k, (where, other) in enumerate(partners):
+            copies.append(
+                remote(source.at[other], target.at[mine], send.at[k], recv.at[k], {"tile": where})
+            )
+            copies[-1].start()
+        return copies
+
+    phase1 = spread_out(out1a, mida, zc, at_zc, p1s.at[0], p1r.at[0])
+    phase1 += spread_out(out1b, midb, yc, at_yc, p1s.at[1], p1r.at[1])
     halos = []
     for where, k in rows:
         for field, source in enumerate((moi, kel)):
@@ -123,17 +134,6 @@
     for copy in halos:
         copy.start()
 
-    def spread_out(source, target, mine, partners, send, recv):
-        copies = []
-        for k, (where, other) in enumerate(partners):
-            copies.append(
-                remote(source.at[other], target.at[mine], send.at[k], recv.at[k], {"tile": where})
-            )
-            copies[-1].start()
-        return copies
-
-    phase1 = spread_out(out1a, mida, zc, at_zc, p1s.at[0], p1r.at[0])
-    phase1 += spread_out(out1b, midb, yc, at_yc, p1s.at[1], p1r.at[1])
     mida[zc] = out1a[zc]
     midb[yc] = out1b[yc]
 
@@ -231,27 +231,28 @@
     for half in range(cols // 128):
         wbuf[half] = chosen[:, 128 * half : 128 * half + 128] * matt_c
 
+    ratio = insol_c / share_c
+    folded = acc.reshape(8 * (levels + 1), 128)
     reduce = []
     for half in range(cols // 128):
         lanes = pl.ds(128 * half, 128)
         w = wbuf[half]
         inv = inv_mu[:, 128 * half : 128 * half + 128]
-        s0 = insol_c * sun[:, 128 * half : 128 * half + 128]
+        s0 = ratio * sun[:, 128 * half : 128 * half + 128]
 
         def down(l, carry, w=w, inv=inv, lanes=lanes):
             d, s = carry
             a = dry[l] + w * q2[jnp.where(l < last, l, l + gap), :, lanes]
             t, u = jnp.exp2(a), jnp.exp2(a * inv)
             m = t * d
+            s = s * u
             tbuf[l] = t
-            mbuf[l] = m
-            s = s * u
-            acc[l + 1] = fold8(s)
+            mbuf[l] = m + s
             return m + dts[l + 1, :, lanes], s
 
         def up(i, e, lanes=lanes):
             l = levels - 1 - i
-            acc[l + 1] += fold8((mbuf[l] - e) * share_c)
+            acc[l + 1] = fold8((mbuf[l] - e) * share_c)
             return tbuf[l] * e + dts_minus(l, lanes)
 
         def dts_minus(l, lanes):
@@ -260,10 +261,10 @@
         start = jnp.broadcast_to(dts[0, :, lanes], (gpts, 128))
         lax.fori_loop(0, levels, down, (start, s0), unroll=10)
         e = lax.fori_loop(0, levels, up, jnp.zeros((gpts, 128), F32), unroll=10)
-        acc[0] = fold8(s0 - share_c * e)
-        total = acc[:, 0, :]
+        acc[0] = fold8((s0 - e) * share_c)
+        total = folded[pl.ds(0, levels + 1, stride=8), :]
         for k in range(1, 8):
-            total = total + acc[:, k, :]
+            total = total + folded[pl.ds(k, levels + 1, stride=8), :]
         flux[...] = total
         gbuf[half, grp] = flux[0:levels, :] - flux[1 : levels + 1, :]
         for k in across:
@@ -275,6 +276,10 @@
             )
             reduce[-1].start()
 
+    for copy in vapour:
+        copy.wait()
+    for copy in halos + shared + phase1 + phase2:
+        copy.wait_send()
     for half in range(cols // 128):
         for copy in reduce[half * (groups - 1) : (half + 1) * (groups - 1)]:
             copy.wait_recv()
@@ -287,9 +292,7 @@
         heat_o[:, :, lanes] = total
         temp_o[0:last, :, lanes] = t2[0:last, :, lanes] + total[0:last]
         temp_o[last:levels, :, lanes] = t2[last + gap : levels + gap, :, lanes] + total[last:levels]
-    for copy in vapour:
-        copy.wait()
-    for copy in halos + shared + phase1 + phase2 + reduce:
+    for copy in reduce:
         copy.wait_send()
 
 

time: 37.3 us -> 35.4 us (0.949)
  the two profiles are of different devices: /device:TPU:1 before, /device:TPU:2 now
where the time goes in v5:
time: 35.4 us; the launch traced here: 35.3 us
  Pallas kernels  34.6 us (98%)
  between operations  0.64 us (2%)
    pallas_call x1, Pallas kernels, on_device(): pl.pallas_call(functools.partial(radiation_kernel, (tiles, ydim, groups))...  33.9 us
    pallas_call x1, Pallas kernels, on_device(): pl.pallas_call(finish_kernel, out_shape=(out, out, out), in_specs=[vmem]...  0.73 us

profile of v5, /device:TPU:2, one launch (start us, length us, event | category | flops | bytes accessed | tf_op | source)
XLA Modules:
  0.0 35.3 jit_solution(10188613081579266931)
XLA Ops:
  0.6 33.9 %shard_map.130 = (f32[90,1,256]{2,1,0:T(1,128)S(1)}, f32[90,1,256]{2,1,0:T(1,128)S(1)}, f32[90,1,256]{2,1,0:T(1,128)S(1)}) custom-call(f32[90,1,256]{2,1,0:T(1,128)} %kel.1, f32[90,1,256]{2,1,0:T(1,128)} %moi.1, f32[1,256]{1,0:T(1,128)} %spread_h.1, f32[1,256]{1,0:T(1,128)} %mu_h.1, s32[1,256]{1,0:T(1,128)} %lit_h.1, s32[1,256]{1,0:T(1,128)} %bitcast.4, ...), custom_call_target="tpu_custom_call" | custom-call | tf_op jit(solution)/shard_map/pallas_call | solution.py:324
  34.5 0.7 %shard_map.131 = (f32[90,1,256]{2,1,0:T(1,128)}, f32[90,1,256]{2,1,0:T(1,128)}, f32[90,1,256]{2,1,0:T(1,128)}) custom-call(f32[90,1,256]{2,1,0:T(1,128)S(1)} %get-tuple-element.6.heat, f32[90,1,256]{2,1,0:T(1,128)S(1)} %get-tuple-element.7.temp, f32[90,1,256]{2,1,0:T(1,128)S(1)} %get-tuple-element.8.vap), custom_call_target="tpu_custom_call" | custom-call | tf_op jit(solution)/shard_map/pallas_call | solution.py:363

commit v6 on v5

--- a/solution.py
+++ b/solution.py
@@ -45,7 +45,7 @@
     facv, spread, mu, lit, owner, arid, matt, share, insol, fact, out1a, out1b, mida, midb, out2a, out2b, gota, gotb, hots,
     mine, halo, coefs, q2, t2, dts,
     dry, tbuf, mbuf, acc, flux, gbuf, wbuf,
-    load_sem, hs, hr, cs, cr, xs, xr, vap_sem, p1s, p1r, p2s, p2r, gs, gr,
+    load_sem, hs, hr, xs, xr, vap_sem, p1s, p1r, p2s, p2r, gs, gr,
 ):
     tiles, ydim, groups = dims
     zcdim, ycdim = tiles // ydim, CORES * ydim
@@ -113,10 +113,11 @@
         copies = []
         for k, (where, other) in enumerate(partners):
             copies.append(
-                remote(source.at[other], target.at[mine], send.at[k], recv.at[k], {"tile": where})
+                remote(source.at[other], target.at[mine], send, recv, {"tile": where})
             )
             copies[-1].start()
-        return copies
+        all_but_one = pl.ds(0, len(partners))
+        return [remote(source.at[all_but_one], target.at[all_but_one], send, recv, {"tile": partners[0][0]})]
 
     phase1 = spread_out(out1a, mida, zc, at_zc, p1s.at[0], p1r.at[0])
     phase1 += spread_out(out1b, midb, yc, at_yc, p1s.at[1], p1r.at[1])
@@ -125,14 +126,19 @@
         for field, source in enumerate((moi, kel)):
             halos.append(
                 remote(
-                    source.at[pl.ds(level, part), 0, :], halo.at[k, field], hs.at[k, field], hr.at[k, field],
+                    source.at[pl.ds(level, part), 0, :], halo.at[k, field], hs.at[0], hr.at[0],
                     {"tile": where},
                 )
             )
         if k in (1, 2):
-            halos.append(remote(spread_h, coefs.at[k - 1], cs.at[k - 1], cr.at[k - 1], {"tile": where}))
+            halos.append(remote(spread_h, coefs.at[k - 1], hs.at[1], hr.at[1], {"tile": where}))
     for copy in halos:
         copy.start()
+    nearby = {"tile": rows[0][0]}
+    halos = [
+        remote(halo, halo, hs.at[0], hr.at[0], nearby),
+        remote(coefs, coefs, hs.at[1], hr.at[1], nearby),
+    ]
 
     mida[zc] = out1a[zc]
     midb[yc] = out1b[yc]
@@ -171,6 +177,16 @@
     def arrive(copies):
         for copy in copies:
             copy.wait_recv()
+
+    arrive(phase1)
+    for k in range(ydim):
+        out2a[k] = mida.reshape(tiles, 2 * SLOT)[pl.ds(k, zcdim, stride=ydim), :]
+    for k in range(zdim):
+        out2b[k] = midb.reshape(tiles, 2 * SLOT)[pl.ds(k, ycdim, stride=zdim), :]
+    phase2 = spread_out(out2a, gota, y, at_y, p2s.at[0], p2r.at[0])
+    phase2 += spread_out(out2b, gotb, z, at_z, p2s.at[1], p2r.at[1])
+    gota[y] = out2a[y]
+    gotb[z] = out2b[z]
 
     loads[1].wait()
     loads[2].wait()
@@ -185,20 +201,11 @@
         here = whole.at[pl.ds(grp * part, part)]
         here[...] = advance(own_row, spread[...], north, south).reshape(part, 1, cols)
         for k in across:
-            shared.append(
-                remote(here, here, xs.at[field, k], xr.at[field, k], {"grp": lax.rem(grp + k, groups)})
-            )
-            shared[-1].start()
-
-    arrive(phase1)
-    for k in range(ydim):
-        out2a[k] = mida.reshape(tiles, 2 * SLOT)[pl.ds(k, zcdim, stride=ydim), :]
-    for k in range(zdim):
-        out2b[k] = midb.reshape(tiles, 2 * SLOT)[pl.ds(k, ycdim, stride=zdim), :]
-    phase2 = spread_out(out2a, gota, y, at_y, p2s.at[0], p2r.at[0])
-    phase2 += spread_out(out2b, gotb, z, at_z, p2s.at[1], p2r.at[1])
-    gota[y] = out2a[y]
-    gotb[z] = out2b[z]
+            remote(here, here, xs.at[field], xr.at[field], {"grp": lax.rem(grp + k, groups)}).start()
+        others = whole.at[pl.ds(0, (groups - 1) * part)]
+        shared.append(
+            remote(others, others, xs.at[field], xr.at[field], {"grp": lax.rem(grp + 1, groups)})
+        )
 
     arrive(shared)
     last = (groups - 1) * part
@@ -268,21 +275,21 @@
         flux[...] = total
         gbuf[half, grp] = flux[0:levels, :] - flux[1 : levels + 1, :]
         for k in across:
-            reduce.append(
-                remote(
-                    gbuf.at[half, grp], gbuf.at[half, grp], gs.at[half, k], gr.at[half, k],
-                    {"grp": lax.rem(grp + k, groups)},
-                )
-            )
-            reduce[-1].start()
+            remote(
+                gbuf.at[half, grp], gbuf.at[half, grp], gs.at[half], gr.at[half],
+                {"grp": lax.rem(grp + k, groups)},
+            ).start()
+        others = gbuf.at[half, pl.ds(0, groups - 1)]
+        reduce.append(
+            remote(others, others, gs.at[half], gr.at[half], {"grp": lax.rem(grp + 1, groups)})
+        )
 
     for copy in vapour:
         copy.wait()
     for copy in halos + shared + phase1 + phase2:
         copy.wait_send()
     for half in range(cols // 128):
-        for copy in reduce[half * (groups - 1) : (half + 1) * (groups - 1)]:
-            copy.wait_recv()
+        reduce[half].wait_recv()
         total = gbuf[half, 0]
         for k in range(1, groups):
             total = total + gbuf[half, k]
@@ -315,7 +322,6 @@
     gpts, slots = fac.shape
     zcdim, ycdim = tiles // ydim, CORES * ydim
     zdim = zcdim // CORES
-    most = max(zcdim, ycdim)
     vmem, hbm = pl.BlockSpec(memory_space=pltpu.VMEM), pl.BlockSpec(memory_space=pltpu.HBM)
     dma = pltpu.SemaphoreType.DMA
     part = -(-levels // (8 * groups)) * 8
@@ -348,9 +354,9 @@
             pltpu.VMEM((levels + 1, 128), F32),
             pltpu.VMEM((cols // 128, groups, levels, 128), F32),
             pltpu.VMEM((cols // 128, gpts, 128), F32),
-            dma((11,)), dma((4, 2)), dma((4, 2)), dma((2,)), dma((2,)), dma((2, groups)), dma((2, groups)), dma((2,)),
-            dma((2, most)), dma((2, most)), dma((2, most)), dma((2, most)),
-            dma((2, groups)), dma((2, groups)),
+            dma((11,)), dma((2,)), dma((2,)), dma((2,)), dma((2,)), dma((2,)),
+            dma((2,)), dma((2,)), dma((2,)), dma((2,)),
+            dma((cols // 128,)), dma((cols // 128,)),
         ],
         compiler_params=pltpu.CompilerParams(
             collective_id=0, has_side_effects=True, vmem_limit_bytes=56 * 2**20

time: 35.4 us -> 33.6 us (0.949)
  Pallas kernels: 34.6 us -> 32.8 us
    pallas_call x1, Pallas kernels: 33.9 us -> 32.1 us  [on_device(): pl.pallas_call(functools.partial(radiation_kernel, (tiles, ydim, groups))...]
where the time goes in v6:
time: 33.6 us; the launch traced here: 33.5 us
  Pallas kernels  32.8 us (98%)
  between operations  0.64 us (2%)
    pallas_call x1, Pallas kernels, on_device(): pl.pallas_call(functools.partial(radiation_kernel, (tiles, ydim, groups))...  32.1 us
    pallas_call x1, Pallas kernels, on_device(): pl.pallas_call(finish_kernel, out_shape=(out, out, out), in_specs=[vmem]...  0.73 us

profile of v6, /device:TPU:2, one launch (start us, length us, event | category | flops | bytes accessed | tf_op | source)
XLA Modules:
  0.0 33.5 jit_solution(14508757503374844617)
XLA Ops:
  0.6 32.1 %shard_map.130 = (f32[90,1,256]{2,1,0:T(1,128)S(1)}, f32[90,1,256]{2,1,0:T(1,128)S(1)}, f32[90,1,256]{2,1,0:T(1,128)S(1)}) custom-call(f32[90,1,256]{2,1,0:T(1,128)} %kel.1, f32[90,1,256]{2,1,0:T(1,128)} %moi.1, f32[1,256]{1,0:T(1,128)} %spread_h.1, f32[1,256]{1,0:T(1,128)} %mu_h.1, s32[1,256]{1,0:T(1,128)} %lit_h.1, s32[1,256]{1,0:T(1,128)} %bitcast.4, ...), custom_call_target="tpu_custom_call" | custom-call | tf_op jit(solution)/shard_map/pallas_call | solution.py:330
  32.8 0.7 %shard_map.131 = (f32[90,1,256]{2,1,0:T(1,128)}, f32[90,1,256]{2,1,0:T(1,128)}, f32[90,1,256]{2,1,0:T(1,128)}) custom-call(f32[90,1,256]{2,1,0:T(1,128)S(1)} %get-tuple-element.6.heat, f32[90,1,256]{2,1,0:T(1,128)S(1)} %get-tuple-element.7.temp, f32[90,1,256]{2,1,0:T(1,128)S(1)} %get-tuple-element.8.vap), custom_call_target="tpu_custom_call" | custom-call | tf_op jit(solution)/shard_map/pallas_call | solution.py:369

commit v7 on v6

--- a/solution.py
+++ b/solution.py
@@ -240,6 +240,8 @@
 
     ratio = insol_c / share_c
     folded = acc.reshape(8 * (levels + 1), 128)
+    cut = levels // 16 * 8 + 8 * (levels > 32)
+    pieces = [(cut, levels), (0, cut)] if 0 < cut < levels else [(0, levels)]
     reduce = []
     for half in range(cols // 128):
         lanes = pl.ds(128 * half, 128)
@@ -266,39 +268,51 @@
             return -dts[l, :, lanes]
 
         start = jnp.broadcast_to(dts[0, :, lanes], (gpts, 128))
-        lax.fori_loop(0, levels, down, (start, s0), unroll=10)
-        e = lax.fori_loop(0, levels, up, jnp.zeros((gpts, 128), F32), unroll=10)
-        acc[0] = fold8((s0 - e) * share_c)
-        total = folded[pl.ds(0, levels + 1, stride=8), :]
-        for k in range(1, 8):
-            total = total + folded[pl.ds(k, levels + 1, stride=8), :]
-        flux[...] = total
-        gbuf[half, grp] = flux[0:levels, :] - flux[1 : levels + 1, :]
-        for k in across:
-            remote(
-                gbuf.at[half, grp], gbuf.at[half, grp], gs.at[half], gr.at[half],
-                {"grp": lax.rem(grp + k, groups)},
-            ).start()
-        others = gbuf.at[half, pl.ds(0, groups - 1)]
-        reduce.append(
-            remote(others, others, gs.at[half], gr.at[half], {"grp": lax.rem(grp + 1, groups)})
-        )
+        lax.fori_loop(0, levels, down, (start, s0), unroll=30)
+        e, done = jnp.zeros((gpts, 128), F32), 0
+        for piece, (low, high) in enumerate(pieces):
+            until = levels - max(low - 1, 0)
+            e = lax.fori_loop(done, until, up, e, unroll=10)
+            done = until
+            if low == 0:
+                acc[0] = fold8((s0 - e) * share_c)
+            total = folded[pl.ds(8 * low, high + 1 - low, stride=8), :]
+            for k in range(1, 8):
+                total = total + folded[pl.ds(8 * low + k, high + 1 - low, stride=8), :]
+            flux[low : high + 1, :] = total
+            lines = pl.ds(low, high - low)
+            gbuf[half, grp, lines] = flux[low:high, :] - flux[low + 1 : high + 1, :]
+            here = gbuf.at[half, grp, lines]
+            for k in across:
+                remote(
+                    here, here, gs.at[half, piece], gr.at[half, piece], {"grp": lax.rem(grp + k, groups)}
+                ).start()
+            others = gbuf.at[half, pl.ds(0, groups - 1), lines]
+            reduce.append(
+                remote(
+                    others, others, gs.at[half, piece], gr.at[half, piece],
+                    {"grp": lax.rem(grp + 1, groups)},
+                )
+            )
 
     for copy in vapour:
         copy.wait()
     for copy in halos + shared + phase1 + phase2:
         copy.wait_send()
     for half in range(cols // 128):
-        reduce[half].wait_recv()
-        total = gbuf[half, 0]
-        for k in range(1, groups):
-            total = total + gbuf[half, k]
         lanes = pl.ds(128 * half, 128)
-        total = total * (1.0 / (groups * gpts))
-        total = total.reshape(levels, 1, 128)
-        heat_o[:, :, lanes] = total
-        temp_o[0:last, :, lanes] = t2[0:last, :, lanes] + total[0:last]
-        temp_o[last:levels, :, lanes] = t2[last + gap : levels + gap, :, lanes] + total[last:levels]
+        for piece, (low, high) in enumerate(pieces):
+            reduce[len(pieces) * half + piece].wait_recv()
+            total = gbuf[half, 0, low:high]
+            for k in range(1, groups):
+                total = total + gbuf[half, k, low:high]
+            total = (total * (1.0 / (groups * gpts))).reshape(high - low, 1, 128)
+            heat_o[low:high, :, lanes] = total
+            for first, stop, shift in ((low, min(high, last), 0), (max(low, last), high, gap)):
+                if first < stop:
+                    temp_o[first:stop, :, lanes] = (
+                        t2[first + shift : stop + shift, :, lanes] + total[first - low : stop - low]
+                    )
     for copy in reduce:
         copy.wait_send()
 
@@ -356,7 +370,7 @@
             pltpu.VMEM((cols // 128, gpts, 128), F32),
             dma((11,)), dma((2,)), dma((2,)), dma((2,)), dma((2,)), dma((2,)),
             dma((2,)), dma((2,)), dma((2,)), dma((2,)),
-            dma((cols // 128,)), dma((cols // 128,)),
+            dma((cols // 128, 2)), dma((cols // 128, 2)),
         ],
         compiler_params=pltpu.CompilerParams(
             collective_id=0, has_side_effects=True, vmem_limit_bytes=56 * 2**20

time: 33.6 us -> 33.3 us (level)
    pallas_call x1, Pallas kernels: 32.1 us -> 31.8 us  [on_device(): pl.pallas_call(functools.partial(radiation_kernel, (tiles, ydim, groups))...]
where the time goes in v7:
time: 33.3 us; the launch traced here: 33.1 us
  Pallas kernels  32.5 us (98%)
  between operations  0.64 us (2%)
    pallas_call x1, Pallas kernels, on_device(): pl.pallas_call(functools.partial(radiation_kernel, (tiles, ydim, groups))...  31.8 us
    pallas_call x1, Pallas kernels, on_device(): pl.pallas_call(finish_kernel, out_shape=(out, out, out), in_specs=[vmem]...  0.73 us

profile of v7, /device:TPU:2, one launch (start us, length us, event | category | flops | bytes accessed | tf_op | source)
XLA Modules:
  0.0 33.1 jit_solution(10333836691816168576)
XLA Ops:
  0.6 31.8 %shard_map.130 = (f32[90,1,256]{2,1,0:T(1,128)S(1)}, f32[90,1,256]{2,1,0:T(1,128)S(1)}, f32[90,1,256]{2,1,0:T(1,128)S(1)}) custom-call(f32[90,1,256]{2,1,0:T(1,128)} %kel.1, f32[90,1,256]{2,1,0:T(1,128)} %moi.1, f32[1,256]{1,0:T(1,128)} %spread_h.1, f32[1,256]{1,0:T(1,128)} %mu_h.1, s32[1,256]{1,0:T(1,128)} %lit_h.1, s32[1,256]{1,0:T(1,128)} %bitcast.4, ...), custom_call_target="tpu_custom_call" | custom-call | tf_op jit(solution)/shard_map/pallas_call | solution.py:344
  32.4 0.7 %shard_map.131 = (f32[90,1,256]{2,1,0:T(1,128)}, f32[90,1,256]{2,1,0:T(1,128)}, f32[90,1,256]{2,1,0:T(1,128)}) custom-call(f32[90,1,256]{2,1,0:T(1,128)S(1)} %get-tuple-element.6.heat, f32[90,1,256]{2,1,0:T(1,128)S(1)} %get-tuple-element.7.temp, f32[90,1,256]{2,1,0:T(1,128)S(1)} %get-tuple-element.8.vap), custom_call_target="tpu_custom_call" | custom-call | tf_op jit(solution)/shard_map/pallas_call | solution.py:383

commit v8 on v7

--- a/solution.py
+++ b/solution.py
@@ -241,7 +241,7 @@
     ratio = insol_c / share_c
     folded = acc.reshape(8 * (levels + 1), 128)
     cut = levels // 16 * 8 + 8 * (levels > 32)
-    pieces = [(cut, levels), (0, cut)] if 0 < cut < levels else [(0, levels)]
+    pieces = [[(0, levels)]] * (cols // 128 - 1) + [[(cut, levels), (0, cut)]]
     reduce = []
     for half in range(cols // 128):
         lanes = pl.ds(128 * half, 128)
@@ -270,8 +270,8 @@
         start = jnp.broadcast_to(dts[0, :, lanes], (gpts, 128))
         lax.fori_loop(0, levels, down, (start, s0), unroll=30)
         e, done = jnp.zeros((gpts, 128), F32), 0
-        for piece, (low, high) in enumerate(pieces):
-            until = levels - max(low - 1, 0)
+        for piece, (low, high) in enumerate(pieces[half]):
+            until = levels if low == 0 else min(-(-(levels + 1 - low) // 10) * 10, levels)
             e = lax.fori_loop(done, until, up, e, unroll=10)
             done = until
             if low == 0:
@@ -301,8 +301,8 @@
         copy.wait_send()
     for half in range(cols // 128):
         lanes = pl.ds(128 * half, 128)
-        for piece, (low, high) in enumerate(pieces):
-            reduce[len(pieces) * half + piece].wait_recv()
+        for piece, (low, high) in enumerate(pieces[half]):
+            reduce[half + piece].wait_recv()
             total = gbuf[half, 0, low:high]
             for k in range(1, groups):
                 total = total + gbuf[half, k, low:high]

time: 33.3 us -> 33.2 us (level)
  no operation moved by 1% of the time
where the time goes in v8:
time: 33.2 us; the launch traced here: 33.1 us
  Pallas kernels  32.5 us (98%)
  between operations  0.64 us (2%)
    pallas_call x1, Pallas kernels, on_device(): pl.pallas_call(functools.partial(radiation_kernel, (tiles, ydim, groups))...  31.7 us
    pallas_call x1, Pallas kernels, on_device(): pl.pallas_call(finish_kernel, out_shape=(out, out, out), in_specs=[vmem]...  0.73 us

profile of v8, /device:TPU:2, one launch (start us, length us, event | category | flops | bytes accessed | tf_op | source)
XLA Modules:
  0.0 33.1 jit_solution(10634113074086062061)
XLA Ops:
  0.6 31.7 %shard_map.130 = (f32[90,1,256]{2,1,0:T(1,128)S(1)}, f32[90,1,256]{2,1,0:T(1,128)S(1)}, f32[90,1,256]{2,1,0:T(1,128)S(1)}) custom-call(f32[90,1,256]{2,1,0:T(1,128)} %kel.1, f32[90,1,256]{2,1,0:T(1,128)} %moi.1, f32[1,256]{1,0:T(1,128)} %spread_h.1, f32[1,256]{1,0:T(1,128)} %mu_h.1, s32[1,256]{1,0:T(1,128)} %lit_h.1, s32[1,256]{1,0:T(1,128)} %bitcast.4, ...), custom_call_target="tpu_custom_call" | custom-call | tf_op jit(solution)/shard_map/pallas_call | solution.py:344
  32.4 0.7 %shard_map.131 = (f32[90,1,256]{2,1,0:T(1,128)}, f32[90,1,256]{2,1,0:T(1,128)}, f32[90,1,256]{2,1,0:T(1,128)}) custom-call(f32[90,1,256]{2,1,0:T(1,128)S(1)} %get-tuple-element.6.heat, f32[90,1,256]{2,1,0:T(1,128)S(1)} %get-tuple-element.7.temp, f32[90,1,256]{2,1,0:T(1,128)S(1)} %get-tuple-element.8.vap), custom_call_target="tpu_custom_call" | custom-call | tf_op jit(solution)/shard_map/pallas_call | solution.py:383

commit v9 on v7

--- a/solution.py
+++ b/solution.py
@@ -178,12 +178,13 @@
         for copy in copies:
             copy.wait_recv()
 
-    arrive(phase1)
+    arrive(phase1[:1])
     for k in range(ydim):
         out2a[k] = mida.reshape(tiles, 2 * SLOT)[pl.ds(k, zcdim, stride=ydim), :]
+    phase2 = spread_out(out2a, gota, y, at_y, p2s.at[0], p2r.at[0])
+    arrive(phase1[1:])
     for k in range(zdim):
         out2b[k] = midb.reshape(tiles, 2 * SLOT)[pl.ds(k, ycdim, stride=zdim), :]
-    phase2 = spread_out(out2a, gota, y, at_y, p2s.at[0], p2r.at[0])
     phase2 += spread_out(out2b, gotb, z, at_z, p2s.at[1], p2r.at[1])
     gota[y] = out2a[y]
     gotb[z] = out2b[z]
@@ -268,7 +269,7 @@
             return -dts[l, :, lanes]
 
         start = jnp.broadcast_to(dts[0, :, lanes], (gpts, 128))
-        lax.fori_loop(0, levels, down, (start, s0), unroll=30)
+        lax.fori_loop(0, levels, down, (start, s0), unroll=45)
         e, done = jnp.zeros((gpts, 128), F32), 0
         for piece, (low, high) in enumerate(pieces):
             until = levels - max(low - 1, 0)

time: 33.3 us -> 33.3 us (level)
  no operation moved by 1% of the time
where the time goes in v9:
time: 33.3 us; the launch traced here: 33.1 us
  Pallas kernels  32.5 us (98%)
  between operations  0.64 us (2%)
    pallas_call x1, Pallas kernels, on_device(): pl.pallas_call(functools.partial(radiation_kernel, (tiles, ydim, groups))...  31.8 us
    pallas_call x1, Pallas kernels, on_device(): pl.pallas_call(finish_kernel, out_shape=(out, out, out), in_specs=[vmem]...  0.73 us

profile of v9, /device:TPU:2, one launch (start us, length us, event | category | flops | bytes accessed | tf_op | source)
XLA Modules:
  0.0 33.1 jit_solution(2504956929268076296)
XLA Ops:
  0.6 31.8 %shard_map.130 = (f32[90,1,256]{2,1,0:T(1,128)S(1)}, f32[90,1,256]{2,1,0:T(1,128)S(1)}, f32[90,1,256]{2,1,0:T(1,128)S(1)}) custom-call(f32[90,1,256]{2,1,0:T(1,128)} %kel.1, f32[90,1,256]{2,1,0:T(1,128)} %moi.1, f32[1,256]{1,0:T(1,128)} %spread_h.1, f32[1,256]{1,0:T(1,128)} %mu_h.1, s32[1,256]{1,0:T(1,128)} %lit_h.1, s32[1,256]{1,0:T(1,128)} %bitcast.4, ...), custom_call_target="tpu_custom_call" | custom-call | tf_op jit(solution)/shard_map/pallas_call | solution.py:345
  32.4 0.7 %shard_map.131 = (f32[90,1,256]{2,1,0:T(1,128)}, f32[90,1,256]{2,1,0:T(1,128)}, f32[90,1,256]{2,1,0:T(1,128)}) custom-call(f32[90,1,256]{2,1,0:T(1,128)S(1)} %get-tuple-element.6.heat, f32[90,1,256]{2,1,0:T(1,128)S(1)} %get-tuple-element.7.temp, f32[90,1,256]{2,1,0:T(1,128)S(1)} %get-tuple-element.8.vap), custom_call_target="tpu_custom_call" | custom-call | tf_op jit(solution)/shard_map/pallas_call | solution.py:384
